TPU v7x, 256 devices: a whole 4x4x8 slice. The times are simulated.
256 devices in a mesh: rows: 16 (over z_hi, y, core), tp: 16 (over x, z_lo).
Axes of the slice: x: 4, y: 4, z: 8 (z_hi: 2, z_lo: 4; z = z_hi * 4 + z_lo), core: 2. Of those that a mesh axis runs over, the one named last changes fastest.
Arguments:
- teacher_hidden: bfloat16 [12288, 8192], P('rows', 'tp'), may hold values from -8 to 8
- norm_gain: float32 [8192], replicated, may hold values from 0.25 to 1.75
- head_weight: bfloat16 [8192, 16384], P('rows', 'tp'), may hold values from -0.19997864 to 0.19997864
- student_logits: bfloat16 [12288, 16384], P('rows', 'tp'), may hold values from -300 to 300
- row_lengths: int32 [3072], P('rows'), may hold values from 1 to 4
Outputs:
- logit_grad: bfloat16 [12288, 16384], P('rows', 'tp')
- loss: float32 [], replicated
All inputs are finite; a program needn't handle non-finite values.
Results may differ from a plain program's by a relative error of at most 0.0049.
Values may be sent and summed in bfloat16 or wider, within the bound.
No kernel may reach another device: no remote copies, remote signals or barrier semaphores. Data moves between devices by JAX's collectives and lax.ppermute only.
A program may use at most 128 MiB of HBM per device.

v0:
```python
import functools
import itertools

import jax
import jax.numpy as jnp
from jax import lax
from jax.experimental import pallas as pl
from jax.experimental.pallas import tpu as pltpu
from jax.sharding import PartitionSpec as P

V = 2048
CB = 8
STEPS = 4
NX = 4
NZ = 4
NY = 4
NH = 2
BLOCKS = 16
CHUNK = 256
MIB = 1 << 20


def tp_at(x, z):
    return x * NZ + z


def row_at(h, y, c):
    return h * 2 * NY + y * 2 + c


def x_ring(d):
    return [(tp_at(x, z), tp_at((x + d) % NX, z)) for x in range(NX) for z in range(NZ)]


def z_ring(d):
    return [(tp_at(x, z), tp_at(x, (z + d) % NZ)) for x in range(NX) for z in range(NZ)]


def y_ring(d):
    return [
        (row_at(h, y, c), row_at(h, (y + d) % NY, c))
        for h in range(NH)
        for y in range(NY)
        for c in range(2)
    ]


def whole(move):
    places = itertools.product(range(NH), range(NY), range(2), range(NX), range(NZ))

    def at(h, y, c, x, z):
        return row_at(h, y, c) * BLOCKS + tp_at(x, z)

    return [(at(*place), at(*move(*place))) for place in places]


def way(c):
    return 1 - 2 * c


def x_first(h, y, c, x, z):
    return h, y, c, (x + way(c)) % NX, z


def x_second(h, y, c, x, z):
    return h, y, c, (x - way(c)) % NX, z


def z_two(h, y, c, x, z):
    there = (h * NZ + z + 2 * way(c)) % (NH * NZ)
    return there // NZ, y, c, x, there % NZ


def row_xor(m):
    return [(r, r ^ m) for r in range(16)]


SAME_HALF = [[row_at(h, y, c) for y in range(NY) for c in range(2)] for h in range(NH)]


def teacher_logits(weight, own, accumulate):
    def first(value):
        return lax.ppermute(value, ("rows", "tp"), whole(x_first))

    def second(value):
        return lax.ppermute(value, ("rows", "tp"), whole(x_second))

    def far_hop(value):
        return lax.ppermute(value, ("rows", "tp"), whole(z_two))

    def z_hop(value, d):
        return lax.ppermute(value, "tp", z_ring(d))

    def widen(shard):
        return lax.all_gather(shard, "rows", axis_index_groups=SAME_HALF)

    near = widen(weight)
    z1 = z_hop(own, 1)
    half_way = far_hop(weight)
    first0, second0 = first(own), second(own)
    third0 = first(first0)

    here1, half_way, own, *_ = lax.optimization_barrier((z1, half_way, own, second0, third0))
    first1, second1 = first(here1), second(here1)
    third1 = first(first1)
    far = far_hop(half_way)

    far, here1, own, *_ = lax.optimization_barrier((far, here1, own, second1, third1))
    far = widen(far)
    z3 = z_hop(own, -1)

    here3, here1 = lax.optimization_barrier((z3, here1))
    z2 = z_hop(here1, 1)
    first3, second3 = first(here3), second(here3)
    groups = [[own, first0, third0, second0], [here1, first1, third1, second1]]
    state = accumulate(0, [groups[0], groups[0], groups[1], groups[1]], near, near)

    here2, on3, *_ = lax.optimization_barrier((z2, second3, first3, state))
    first2, third3 = first(here2), second(on3)

    here2, on2, *_ = lax.optimization_barrier((here2, first2, third3))
    second2, third2 = second(here2), first(on2)
    blocks = [groups[0], groups[0], groups[1], groups[1]]
    blocks += [[one] for one in (here3, first3, second3, third3, here2, first2)]
    state = accumulate(4, blocks, near, far, state)
    return accumulate(14, [[second2], [third2]], near, far, state)


ORDER = [(0, None), (0, None), (1, None), (1, None)] * 2
ORDER += [(3, 0), (3, 1), (3, 3), (3, 2), (2, 0), (2, 1), (2, 3), (2, 2)]


def block_plan():
    tp = lax.axis_index("tp")
    row = lax.axis_index("rows")
    half = row // 8
    turn = way(row % 2)
    x, z = tp // NZ, tp % NZ
    offsets, blocks, slots = [], [], []
    for step, (i, off) in enumerate(ORDER):
        if off is None:
            side = half if step < 4 else 1 - half
            off = ((x - (2 * side + step % 2)) * turn) % NX
        block = ((x - off * turn) % NX) * NZ + (z - i) % NZ
        offsets.append(jnp.asarray(off, jnp.int32))
        blocks.append(block)
        slots.append(jnp.where(block // 8 == half, block % 8, 8 + block % 8))
    return jnp.stack(slots + blocks + offsets).astype(jnp.int32)


def teacher_kernel(first, choices, plan_ref, gain_ref, near_ref, far_ref, *refs):
    refs = list(refs)
    count = len(choices)
    last = first + count == BLOCKS
    student_ref = refs.pop(0) if last else None
    state_ref = refs.pop(0) if first else None
    blocks = [[refs.pop(0) for _ in range(n)] for n in choices]
    out_ref = refs.pop(0)
    stats_ref = refs.pop(0) if last else None
    total_ref, a_vm, w_vm, a_sem, w_sem, state_sem, *extra = refs
    tok, width = total_ref.shape
    cols = width - 128

    def start(step):
        for off, block in enumerate(blocks[step]):
            wanted = plan_ref[2 * BLOCKS + first + step] == off if len(blocks[step]) > 1 else True

            @pl.when(wanted)
            def _():
                pltpu.make_async_copy(block, a_vm.at[step], a_sem.at[step]).start()

        slot = plan_ref[first + step]

        @pl.when(slot < 8)
        def _():
            pltpu.make_async_copy(near_ref.at[slot], w_vm.at[step], w_sem.at[step]).start()

        @pl.when(slot >= 8)
        def _():
            pltpu.make_async_copy(far_ref.at[slot - 8], w_vm.at[step], w_sem.at[step]).start()

    def multiply(step, r, more=None):
        rows = slice(r, r + CHUNK)
        wide = a_vm[step, rows, :].astype(jnp.float32)
        square = wide * wide
        square = square[:, :128] + square[:, 128:256] + square[:, 256:384] + square[:, 384:]
        normed = (wide * gain_ref[plan_ref[BLOCKS + first + step]]).astype(jnp.bfloat16)
        total = jnp.dot(normed, w_vm[step], preferred_element_type=jnp.float32)
        if more is not None:
            total += more[rows, :cols]
            square += more[rows, cols:]
        return rows, total, square

    def arrive(step):
        pltpu.make_async_copy(a_vm.at[step], a_vm.at[step], a_sem.at[step]).wait()
        pltpu.make_async_copy(w_vm.at[step], w_vm.at[step], w_sem.at[step]).wait()

    def whole_step(step, carry):
        arrive(step)
        for later in range(2, count):

            @pl.when(step + 2 == later)
            def _():
                start(later)

        for r in range(0, tok, CHUNK):
            rows, total, square = multiply(step, r, total_ref)
            total_ref[rows, :cols] = total
            total_ref[rows, cols:] = square
        return carry

    start(0)
    if last:
        state_vm, stud_vm, stud_sem = extra
        student = pltpu.make_async_copy(student_ref, stud_vm, stud_sem)
        state = pltpu.make_async_copy(state_ref.at[pl.ds(0, tok)], state_vm, state_sem)
        start(1)
        state.start()
        student.start()
        arrive(0)
        for r in range(0, tok, CHUNK):
            rows, total, square = multiply(0, r)
            total_ref[rows, :cols] = total
            total_ref[rows, cols:] = square
        arrive(1)
        state.wait()
        student.wait()
        for r in range(0, tok, CHUNK):
            rows, total, square = multiply(1, r, total_ref)
            total += state_vm[rows, :cols]
            square += state_vm[rows, cols:]
            stats_ref[:, rows] = statistics(total, square, stud_vm[rows, :], out_ref, rows)
        return
    if first:
        state = pltpu.make_async_copy(state_ref.at[pl.ds(0, tok)], total_ref, state_sem)
        state.start()
        start(1)
        state.wait()
    else:
        start(1)
        total_ref[...] = jnp.zeros_like(total_ref)
    lax.fori_loop(0, count, whole_step, 0)
    result = pltpu.make_async_copy(total_ref, out_ref.at[pl.ds(0, tok)], state_sem)
    result.start()
    result.wait()


def statistics(logits, square, student, out_ref, rows):
    mean = jnp.sum(square, axis=1, keepdims=True) / (BLOCKS * 512)
    teach = logits * lax.rsqrt(mean + 1e-05)
    out_ref[rows, :] = teach
    stud = student.astype(jnp.float32)
    teach_peak = jnp.max(teach, axis=1, keepdims=True)
    stud_peak = jnp.max(stud, axis=1, keepdims=True)
    teach = teach - teach_peak
    stud = stud - stud_peak
    mass = jnp.exp(stud)
    teach_total = jnp.sum(jnp.exp(teach), axis=1, keepdims=True)
    stud_total = jnp.sum(mass, axis=1, keepdims=True)
    cross = jnp.sum(mass * (stud - teach), axis=1, keepdims=True)
    lane = lax.broadcasted_iota(jnp.int32, (CHUNK, 128), 1)
    packed = jnp.zeros((CHUNK, 128), jnp.float32)
    for at, value in enumerate((teach_peak, teach_total, stud_peak, stud_total, cross)):
        packed = jnp.where(lane == at, value, packed)
    return packed.T[:8, :]


def accumulate_blocks(gain, student, plan, first, blocks, near, far, state=None):
    tok, cols = student.shape
    hbm = pl.BlockSpec(memory_space=pltpu.HBM)
    vmem = pl.BlockSpec(memory_space=pltpu.VMEM)
    smem = pl.BlockSpec(memory_space=pltpu.SMEM)
    anywhere = pl.BlockSpec(memory_space=pl.ANY)
    logits = jax.ShapeDtypeStruct((tok, cols), jnp.float32)
    totals = jax.ShapeDtypeStruct((8 * tok, cols + 128), jnp.float32)
    stats = jax.ShapeDtypeStruct((8, tok), jnp.float32)
    count = len(blocks)
    last = first + count == BLOCKS
    scratch = [
        pltpu.VMEM((tok, cols + 128), jnp.float32),
        pltpu.VMEM((count, tok, 512), jnp.bfloat16),
        pltpu.VMEM((count, 512, cols), jnp.bfloat16),
        pltpu.SemaphoreType.DMA((count,)),
        pltpu.SemaphoreType.DMA((count,)),
        pltpu.SemaphoreType.DMA,
    ]
    if last:
        scratch += [
            pltpu.VMEM((tok, cols + 128), jnp.float32),
            pltpu.VMEM((tok, cols), jnp.bfloat16),
            pltpu.SemaphoreType.DMA,
        ]
    parts = [student] * last + [state] * (first > 0) + [one for block in blocks for one in block]
    return pl.pallas_call(
        functools.partial(teacher_kernel, first, [len(block) for block in blocks]),
        out_shape=(logits, stats) if last else totals,
        in_specs=[smem, vmem] + [hbm] * 2 + [anywhere] * len(parts),
        out_specs=(vmem, vmem) if last else hbm,
        scratch_shapes=scratch,
        compiler_params=pltpu.CompilerParams(vmem_limit_bytes=(42 if last else 60) * MIB),
        name="teacher_" + str(first),
    )(plan, gain.reshape(BLOCKS, 1, 512), near, far, *parts)


def merge(first, second):
    teach_peak = jnp.maximum(first[0], second[0])
    stud_peak = jnp.maximum(first[2], second[2])
    teach_total = stud_total = cross = 0.0
    for part in (first, second):
        teach_low = part[0] - teach_peak
        stud_low = part[2] - stud_peak
        weight = jnp.exp(stud_low)
        teach_total = teach_total + jnp.exp(teach_low) * part[1]
        stud_total = stud_total + weight * part[3]
        cross = cross + weight * (part[4] + part[3] * (stud_low - teach_low))
    log_stud = jnp.log(stud_total)
    log_teach = jnp.log(teach_total)
    divergence = cross / stud_total - (log_stud - log_teach)
    offset = (stud_peak - teach_peak) + (log_stud - log_teach) + divergence
    return stud_peak, log_stud, offset, divergence


def combine_kernel(own_ref, near_ref, third_ref, fourth_ref, live_ref, count_ref, coef_ref, sums_ref):
    parts = [
        [ref[at : at + 1, :] for at in range(5)]
        for ref in (own_ref, near_ref, third_ref, fourth_ref)
    ]
    live = live_ref[...]
    stud_peak, log_stud, offset, divergence = merge(parts[0], parts[1])
    other_divergence = merge(parts[2], parts[3])[3]
    coef_ref[...] = jnp.zeros_like(coef_ref)
    coef_ref[0:1, :] = stud_peak
    coef_ref[1:2, :] = log_stud
    coef_ref[2:3, :] = offset
    coef_ref[3:4, :] = V * live
    lane = lax.broadcasted_iota(jnp.int32, (1, 128), 1)
    total = jnp.sum(live * (divergence + other_divergence), axis=1, keepdims=True)
    sums_ref[...] = jnp.where(lane == 0, total, jnp.where(lane == 1, count_ref[0], 0.0))


def combine(stats, others, live, count):
    vmem = pl.BlockSpec(memory_space=pltpu.VMEM)
    return pl.pallas_call(
        combine_kernel,
        out_shape=(
            jax.ShapeDtypeStruct(stats.shape, jnp.float32),
            jax.ShapeDtypeStruct((1, 128), jnp.float32),
        ),
        in_specs=[vmem] * 5 + [pl.BlockSpec(memory_space=pltpu.SMEM)],
        out_specs=(vmem, vmem),
        compiler_params=pltpu.CompilerParams(vmem_limit_bytes=4 * MIB),
        name="combine",
    )(stats, *others, live, count)


def grad_kernel(coef_ref, teach_ref, student_ref, grad_ref):
    coef = coef_ref[...].T
    stud = student_ref[...].astype(jnp.float32)
    prob = jnp.exp((stud - coef[:, 0:1]) - coef[:, 1:2])
    differ = (stud - teach_ref[...]) - coef[:, 2:3]
    grad_ref[...] = ((coef[:, 3:4] * prob) * differ).astype(jnp.bfloat16)


def gradient(coef, teach, student):
    tok, cols = student.shape
    tile = 384
    rows = pl.BlockSpec((tile, cols), lambda i: (i, 0))
    return pl.pallas_call(
        grad_kernel,
        grid=(tok // tile,),
        out_shape=jax.ShapeDtypeStruct((tok, cols), jnp.bfloat16),
        in_specs=[pl.BlockSpec((8, tile), lambda i: (0, i)), rows, rows],
        out_specs=rows,
        compiler_params=pltpu.CompilerParams(vmem_limit_bytes=24 * MIB),
        name="gradient",
    )(coef, teach, student)


def stage(value, axis, moves):
    return sum([lax.ppermute(value, axis, move) for move in moves], value)


def body(teacher_hidden, norm_gain, head_weight, student_logits, row_lengths):
    tok = teacher_hidden.shape[0]
    steps_of = jnp.arange(tok, dtype=jnp.int32) % STEPS
    live = (steps_of < jnp.repeat(row_lengths, STEPS)).astype(jnp.float32)
    count = jnp.sum(row_lengths.astype(jnp.float32))
    accumulate = functools.partial(accumulate_blocks, norm_gain, student_logits, block_plan())
    teach, stats = teacher_logits(head_weight, teacher_hidden, accumulate)
    others = [
        lax.ppermute(stats, "tp", [(t, t ^ m) for t in range(BLOCKS)]) for m in (1, 2, 3)
    ]
    coef, sums = combine(stats, others, live.reshape(1, tok), count.reshape(1))

    sums = stage(sums, "rows", [row_xor(1)])
    sums = stage(sums, "rows", [row_xor(8)])
    grad = gradient(coef, teach, student_logits)
    sums, grad = lax.optimization_barrier((sums, grad))
    sums = stage(sums, "rows", [y_ring(d) for d in (1, 2, 3)])
    sums = stage(sums, "tp", [x_ring(d) for d in (1, 2, 3)])
    loss = sums[0, 0] / (CB * (sums[0, 1] / NX))
    return (grad, loss)


def solution(mesh):
    in_specs = (P("rows", "tp"), P(), P("rows", "tp"), P("rows", "tp"), P("rows"))
    out_specs = (P("rows", "tp"), P())
    return jax.shard_map(body, mesh=mesh, in_specs=in_specs, out_specs=out_specs, check_vma=False)
```

profile of v0, /device:TPU:2, one launch (start us, length us, event | category | flops | bytes accessed | tf_op | source)
XLA Modules:
  0.0 211.5 jit_solution(17485460121623649448)
XLA Ops:
  7.2 0.0 all-gather.5.cloned.1.call-start
  7.2 0.7 all-gather.5.cloned.1.call-update
  7.9 0.0 all-gather.7.cloned.1.call-start
  7.9 1.6 collective-permute-start.3
  9.5 3.3 %collective-permute-start.1 = (bf16[512,1024]{1,0:T(8,128)(2,1)}, bf16[512,1024]{1,0:T(8,128)(2,1)S(1)}, u32[]{:S(2)}, u32[]{:S(2)}) collective-permute-start(bf16[512,1024]{1,0:T(8,128)(2,1)} %param.7), channel_id=1, source_target_pairs={{0,2},{1,3},{2,128},{3,129},{4,6},{5,7},{6,132},{7,133},{8,10},{9,... | collective-permute-start | bytes 3145736 | tf_op jit(solution)/shard_map/ppermute | solution.py:89
  12.8 0.5 collective-permute-start.2
  13.3 1.9 collective-permute-start
  15.2 7.7 %collective-permute-done.3.refs_1_.refs_5_.refs_2_.refs_6_ = bf16[768,512]{1,0:T(8,128)(2,1)S(1)} collective-permute-done((bf16[768,512]{1,0:T(8,128)(2,1)}, bf16[768,512]{1,0:T(8,128)(2,1)S(1)}, u32[]{:S(2)}, u32[]{:S(2)}) %collective-permute-start.3) | collective-permute-done | bytes 786464 | tf_op jit(solution)/shard_map/ppermute | solution.py:83
  22.9 2.0 collective-permute-start.4
  24.9 5.8 %collective-permute-done.2.refs_3_.refs_7_.refs_4_.refs_8_ = bf16[768,512]{1,0:T(8,128)(2,1)S(1)} collective-permute-done((bf16[768,512]{1,0:T(8,128)(2,1)}, bf16[768,512]{1,0:T(8,128)(2,1)S(1)}, u32[]{:S(2)}, u32[]{:S(2)}) %collective-permute-start.2) | collective-permute-done | bytes 786464 | tf_op jit(solution)/shard_map/ppermute | solution.py:86
  30.7 22.8 %collective-permute-done.refs_8_.refs_12_.refs_9_.refs_13_ = bf16[768,512]{1,0:T(8,128)(2,1)S(1)} collective-permute-done((bf16[768,512]{1,0:T(8,128)(2,1)}, bf16[768,512]{1,0:T(8,128)(2,1)S(1)}, u32[]{:S(2)}, u32[]{:S(2)}) %collective-permute-start) | collective-permute-done | bytes 786464 | tf_op jit(solution)/shard_map/ppermute | solution.py:92
  53.5 1.3 collective-permute-start.7
  54.8 3.3 %collective-permute-start.5 = (bf16[512,1024]{1,0:T(8,128)(2,1)S(1)}, bf16[512,1024]{1,0:T(8,128)(2,1)}, u32[]{:S(2)}, u32[]{:S(2)}) collective-permute-start(bf16[512,1024]{1,0:T(8,128)(2,1)S(1)} %collective-permute-done.1), channel_id=1, source_target_pairs={{0,2},{1,3},{2,128},{3,129},{4,6},{5,7},{6,132},{7,133},{8,10},{9,... | collective-permute-start | bytes 3145736 | tf_op jit(solution)/shard_map/ppermute | solution.py:89
  58.1 0.8 collective-permute-start.6
  58.9 14.0 %collective-permute-done.7.refs_9_.refs_13_.refs_10_.refs_14_ = bf16[768,512]{1,0:T(8,128)(2,1)} collective-permute-done((bf16[768,512]{1,0:T(8,128)(2,1)S(1)}, bf16[768,512]{1,0:T(8,128)(2,1)}, u32[]{:S(2)}, u32[]{:S(2)}) %collective-permute-start.7) | collective-permute-done | bytes 786464 | tf_op jit(solution)/shard_map/ppermute | solution.py:83
  72.9 2.2 %collective-permute-start.8 = (bf16[768,512]{1,0:T(8,128)(2,1)}, bf16[768,512]{1,0:T(8,128)(2,1)}, u32[]{:S(2)}, u32[]{:S(2)}) collective-permute-start(bf16[768,512]{1,0:T(8,128)(2,1)} %collective-permute-done.7.refs_9_.refs_13_.refs_10_.refs_14_), channel_id=1, source_target_pairs={{0,4},{1,5},{2,6},{3,7},{4,8},{5,9},{6,10},{7,11},{8,12},{9,13},{1... | collective-permute-start | bytes 2359304 | tf_op jit(solution)/shard_map/ppermute | solution.py:83
  75.0 0.0 collective-permute-done.6.refs_11_.refs_15_.refs_12_.refs_16_
  75.0 0.9 copy-done.7
  76.0 7.8 %collective-permute-done.5 = bf16[512,1024]{1,0:T(8,128)(2,1)} collective-permute-done((bf16[512,1024]{1,0:T(8,128)(2,1)S(1)}, bf16[512,1024]{1,0:T(8,128)(2,1)}, u32[]{:S(2)}, u32[]{:S(2)}) %collective-permute-start.5) | collective-permute-done | bytes 1048608 | tf_op jit(solution)/shard_map/ppermute | solution.py:89
  83.7 1.4 collective-permute-done.8.refs_10_.refs_14_.refs_11_.refs_15_
  85.2 0.0 all-gather.7.cloned.1.call-update
  85.2 4.2 %collective-permute-start.9 = (bf16[768,512]{1,0:T(8,128)(2,1)}, bf16[768,512]{1,0:T(8,128)(2,1)}, u32[]{:S(2)}, u32[]{:S(2)}) collective-permute-start(bf16[768,512]{1,0:T(8,128)(2,1)} %refs_5_), channel_id=1, source_target_pairs={{0,3},{1,0},{2,1},{3,2},{4,7},{5,4},{6,5},{7,6},{8,11},{9,8},{10,9... | collective-permute-start | bytes 2359304 | tf_op jit(solution)/shard_map/ppermute | solution.py:92
  89.4 12.5 %collective-permute-done.9.refs_17_ = bf16[768,512]{1,0:T(8,128)(2,1)} collective-permute-done((bf16[768,512]{1,0:T(8,128)(2,1)}, bf16[768,512]{1,0:T(8,128)(2,1)}, u32[]{:S(2)}, u32[]{:S(2)}) %collective-permute-start.9) | collective-permute-done | bytes 786464 | tf_op jit(solution)/shard_map/ppermute | solution.py:92
  101.9 0.9 collective-permute-start.10
  102.8 1.3 collective-permute-start.11
  104.0 1.1 collective-permute-start.12
  105.2 0.7 stack.151.plan_ref
  105.9 0.0 copy-start.10
  105.9 8.1 %teacher_0.1.refs_0_ = f32[6144,1152]{1,0:T(8,128)} custom-call(s32[48]{0:T(128)} %stack.151.plan_ref, f32[16,1,512]{2,1,0:T(1,128)} %bitcast.41, bf16[8,512,1024]{2,1,0:T(8,128)(2,1)} %bitcast.44, bf16[8,512,1024]{2,1,0:T(8,128)(2,1)} %bitcast.45, bf16[768,512]{1,0:T(8,128)(2,1)} %refs_5_, bf16[768,512]{1,0:T(8,128)(2,1)} %copy-done.3, ...), custom_call_target="tpu_custom_call" | custom-call | tf_op jit(solution)/shard_map/teacher_0/pallas_call | solution.py:294
  114.0 6.6 %collective-permute-done.10.refs_18_ = bf16[768,512]{1,0:T(8,128)(2,1)} collective-permute-done((bf16[768,512]{1,0:T(8,128)(2,1)}, bf16[768,512]{1,0:T(8,128)(2,1)}, u32[]{:S(2)}, u32[]{:S(2)}) %collective-permute-start.10) | collective-permute-done | bytes 786464 | tf_op jit(solution)/shard_map/ppermute | solution.py:83
  120.7 3.3 %collective-permute-start.13 = (bf16[768,512]{1,0:T(8,128)(2,1)}, bf16[768,512]{1,0:T(8,128)(2,1)S(1)}, u32[]{:S(2)}, u32[]{:S(2)}) collective-permute-start(bf16[768,512]{1,0:T(8,128)(2,1)} %collective-permute-done.11.refs_19_), channel_id=1, source_target_pairs={{0,12},{1,13},{2,14},{3,15},{4,0},{5,1},{6,2},{7,3},{8,4},{9,5},{1... | collective-permute-start | bytes 2359304 | tf_op jit(solution)/shard_map/ppermute | solution.py:86
  124.0 16.5 %collective-permute-done.13.refs_20_ = bf16[768,512]{1,0:T(8,128)(2,1)S(1)} collective-permute-done((bf16[768,512]{1,0:T(8,128)(2,1)}, bf16[768,512]{1,0:T(8,128)(2,1)S(1)}, u32[]{:S(2)}, u32[]{:S(2)}) %collective-permute-start.13) | collective-permute-done | bytes 786464 | tf_op jit(solution)/shard_map/ppermute | solution.py:86
  140.5 0.0 collective-permute-done.14.refs_22_
  140.5 0.9 copy-done.9
  141.4 1.0 collective-permute-start.15
  142.4 1.0 collective-permute-start.16
  143.4 0.1 broadcast_in_dim.3
  143.5 0.1 reshape.55
  143.6 0.0 all-gather.7.cloned.1.call-done
  143.7 0.0 copy-start
  143.7 0.0 copy-start.1
  143.7 16.0 %teacher_4.1.refs_1_ = f32[6144,1152]{1,0:T(8,128)} custom-call(s32[48]{0:T(128)} %stack.151.plan_ref, f32[16,1,512]{2,1,0:T(1,128)} %bitcast.42, bf16[8,512,1024]{2,1,0:T(8,128)(2,1)} %bitcast.46, bf16[8,512,1024]{2,1,0:T(8,128)(2,1)} %bitcast.48, f32[6144,1152]{1,0:T(8,128)} %teacher_0.1.refs_0_, bf16[768,512]{1,0:T(8,128)(2,1)} %refs_5_, ...), custom_call_target="tpu_custom_call" | custom-call | tf_op jit(solution)/shard_map/teacher_4/pallas_call | solution.py:294
  159.7 0.0 collective-permute-done.16.refs_3_
  159.8 6.0 %teacher_14.1 = (f32[768,1024]{1,0:T(8,128)S(1)}, f32[8,768]{1,0:T(8,128)S(1)}) custom-call(s32[48]{0:T(128)S(1)} %copy-done.2, f32[16,1,512]{2,1,0:T(1,128)S(1)} %bitcast.43, bf16[8,512,1024]{2,1,0:T(8,128)(2,1)} %bitcast.47, bf16[8,512,1024]{2,1,0:T(8,128)(2,1)} %bitcast.49, bf16[768,1024]{1,0:T(8,128)(2,1)S(1)} %copy-done, ...), custom_call_target="tpu_custom_call" | custom-call | tf_op jit(solution)/shard_map/teacher_14/pallas_call | solution.py:294
  165.8 0.1 collective-permute-start.17
  165.9 0.2 collective-permute-start.18
  166.1 4.2 %collective-permute-start.19 = (f32[8,768]{1,0:T(8,128)S(1)}, f32[8,768]{1,0:T(8,128)S(1)}, u32[]{:S(2)}, u32[]{:S(2)}) collective-permute-start(f32[8,768]{1,0:T(8,128)S(1)} %get-tuple-element.32.own_ref), channel_id=1, source_target_pairs={{0,3},{1,2},{2,1},{3,0},{4,7},{5,6},{6,5},{7,4},{8,11},{9,10},{10,... | collective-permute-start | bytes 73736 | tf_op jit(solution)/shard_map/ppermute | solution.py:391
  170.2 0.6 convert_reduce_fusion
  170.8 1.5 collective-permute-done.19.fourth_ref
  172.3 0.8 combine.1
  173.0 0.0 collective-permute-start.20
  173.1 1.1 collective-permute-done.20
  174.2 8.3 %collective-permute-start.21 = (f32[1,128]{1,0:T(1,128)S(1)}, f32[1,128]{1,0:T(1,128)S(1)}, u32[]{:S(2)}, u32[]{:S(2)}) collective-permute-start(f32[1,128]{1,0:T(1,128)S(1)} %add.374), channel_id=1, source_target_pairs={{0,128},{16,144},{32,160},{48,176},{64,192},{80,208},{96,224},{112... | collective-permute-start | bytes 1544 | tf_op jit(solution)/shard_map/ppermute | solution.py:380
  182.5 2.6 %gradient.1 = bf16[768,1024]{1,0:T(8,128)(2,1)} custom-call(f32[8,768]{1,0:T(8,128)S(1)} %get-tuple-element.34.coef_ref, f32[768,1024]{1,0:T(8,128)S(1)} %get-tuple-element.35.teach_ref, bf16[768,1024]{1,0:T(8,128)(2,1)S(1)} %copy-done), custom_call_target="tpu_custom_call" | custom-call | tf_op jit(solution)/shard_map/gradient/pallas_call | solution.py:368
  185.1 1.0 collective-permute-start.22
  186.1 3.5 %collective-permute-start.23 = (f32[1,128]{1,0:T(1,128)S(1)}, f32[1,128]{1,0:T(1,128)S(1)}, u32[]{:S(2)}, u32[]{:S(2)}) collective-permute-start(f32[1,128]{1,0:T(1,128)S(1)} %add.375), channel_id=1, source_target_pairs={{0,64},{16,80},{32,96},{48,112},{64,0},{80,16},{96,32},{112,48},{1... | collective-permute-start | bytes 1544 | tf_op jit(solution)/shard_map/ppermute | solution.py:380
  189.6 0.8 collective-permute-start.24
  190.4 0.8 collective-permute-done.23
  191.2 2.0 collective-permute-done.24
  193.1 1.9 collective-permute-start.25
  195.0 2.8 %collective-permute-start.26 = (f32[1,128]{1,0:T(1,128)S(1)}, f32[1,128]{1,0:T(1,128)S(1)}, u32[]{:S(2)}, u32[]{:S(2)}) collective-permute-start(f32[1,128]{1,0:T(1,128)S(1)} %add_add_fusion.1), channel_id=1, source_target_pairs={{0,8},{1,9},{2,10},{3,11},{4,12},{5,13},{6,14},{7,15},{8,0},{9,1},... | collective-permute-start | bytes 1544 | tf_op jit(solution)/shard_map/ppermute | solution.py:380
  197.8 2.5 %collective-permute-start.27 = (f32[1,128]{1,0:T(1,128)S(1)}, f32[1,128]{1,0:T(1,128)S(1)}, u32[]{:S(2)}, u32[]{:S(2)}) collective-permute-start(f32[1,128]{1,0:T(1,128)S(1)} %add_add_fusion.1), channel_id=1, source_target_pairs={{0,12},{1,13},{2,14},{3,15},{4,0},{5,1},{6,2},{7,3},{8,4},{9,5},{1... | collective-permute-start | bytes 1544 | tf_op jit(solution)/shard_map/ppermute | solution.py:380
  200.4 1.3 collective-permute-done.27
  201.6 0.6 fusion
  (35 shorter events, 0.1 us)
Async XLA Ops:
  7.2 98.7 %all-gather.5.cloned.1.call-start = ((), (), s32[]{:S(2)}) async-start(), calls=%async_computation | async-start | bytes 9437184 | tf_op jit(solution)/shard_map/all_gather | solution.py:95
  7.9 135.8 %all-gather.7.cloned.1.call-start = ((), (), s32[]{:S(2)}) async-start(), calls=%async_computation.1 | async-start | bytes 9437184 | tf_op jit(solution)/shard_map/all_gather | solution.py:95
  7.9 15.0 %collective-permute-start.3 = (bf16[768,512]{1,0:T(8,128)(2,1)}, bf16[768,512]{1,0:T(8,128)(2,1)S(1)}, u32[]{:S(2)}, u32[]{:S(2)}) collective-permute-start(bf16[768,512]{1,0:T(8,128)(2,1)} %refs_5_), channel_id=1, source_target_pairs={{0,4},{1,5},{2,6},{3,7},{4,8},{5,9},{6,10},{7,11},{8,12},{9,13},{1... | collective-permute-start | bytes 2359304 | tf_op jit(solution)/shard_map/ppermute | solution.py:83
  9.5 44.0 %collective-permute-start.1 = (bf16[512,1024]{1,0:T(8,128)(2,1)}, bf16[512,1024]{1,0:T(8,128)(2,1)S(1)}, u32[]{:S(2)}, u32[]{:S(2)}) collective-permute-start(bf16[512,1024]{1,0:T(8,128)(2,1)} %param.7), channel_id=1, source_target_pairs={{0,2},{1,3},{2,128},{3,129},{4,6},{5,7},{6,132},{7,133},{8,10},{9,... | collective-permute-start | bytes 3145736 | tf_op jit(solution)/shard_map/ppermute | solution.py:89
  12.8 17.9 %collective-permute-start.2 = (bf16[768,512]{1,0:T(8,128)(2,1)}, bf16[768,512]{1,0:T(8,128)(2,1)S(1)}, u32[]{:S(2)}, u32[]{:S(2)}) collective-permute-start(bf16[768,512]{1,0:T(8,128)(2,1)} %refs_5_), channel_id=1, source_target_pairs={{0,12},{1,13},{2,14},{3,15},{4,0},{5,1},{6,2},{7,3},{8,4},{9,5},{1... | collective-permute-start | bytes 2359304 | tf_op jit(solution)/shard_map/ppermute | solution.py:86
  13.3 40.2 %collective-permute-start = (bf16[768,512]{1,0:T(8,128)(2,1)}, bf16[768,512]{1,0:T(8,128)(2,1)S(1)}, u32[]{:S(2)}, u32[]{:S(2)}) collective-permute-start(bf16[768,512]{1,0:T(8,128)(2,1)} %refs_5_), channel_id=1, source_target_pairs={{0,1},{1,2},{2,3},{3,0},{4,5},{5,6},{6,7},{7,4},{8,9},{9,10},{10,1... | collective-permute-start | bytes 2359304 | tf_op jit(solution)/shard_map/ppermute | solution.py:92
  22.9 83.0 %copy-start.3 = (bf16[768,512]{1,0:T(8,128)(2,1)}, bf16[768,512]{1,0:T(8,128)(2,1)S(1)}, u32[]{:S(2)}) copy-start(bf16[768,512]{1,0:T(8,128)(2,1)S(1)} %collective-permute-done.3.refs_1_.refs_5_.refs_2_.refs_6_) | copy-start | bytes 2359300
  22.9 30.6 %collective-permute-start.4 = (bf16[768,512]{1,0:T(8,128)(2,1)S(1)}, bf16[768,512]{1,0:T(8,128)(2,1)S(1)}, u32[]{:S(2)}, u32[]{:S(2)}) collective-permute-start(bf16[768,512]{1,0:T(8,128)(2,1)S(1)} %collective-permute-done.3.refs_1_.refs_5_.refs_2_.refs_6_), channel_id=1, source_target_pairs={{0,4},{1,5},{2,6},{3,7},{4,8},{5,9},{6,10},{7,11},{8,12},{9,13},{1... | collective-permute-start | bytes 2359304 | tf_op jit(solution)/shard_map/ppermute | solution.py:83
  30.7 75.2 %copy-start.4 = (bf16[768,512]{1,0:T(8,128)(2,1)}, bf16[768,512]{1,0:T(8,128)(2,1)S(1)}, u32[]{:S(2)}) copy-start(bf16[768,512]{1,0:T(8,128)(2,1)S(1)} %collective-permute-done.2.refs_3_.refs_7_.refs_4_.refs_8_) | copy-start | bytes 2359300
  53.5 52.4 %copy-start.5 = (bf16[768,512]{1,0:T(8,128)(2,1)}, bf16[768,512]{1,0:T(8,128)(2,1)S(1)}, u32[]{:S(2)}) copy-start(bf16[768,512]{1,0:T(8,128)(2,1)S(1)} %collective-permute-done.refs_8_.refs_12_.refs_9_.refs_13_) | copy-start | bytes 2359300
  53.5 52.4 %copy-start.6 = (bf16[768,512]{1,0:T(8,128)(2,1)}, bf16[768,512]{1,0:T(8,128)(2,1)S(1)}, u32[]{:S(2)}) copy-start(bf16[768,512]{1,0:T(8,128)(2,1)S(1)} %collective-permute-done.4.refs_2_.refs_6_.refs_3_.refs_7_) | copy-start | bytes 2359300
  53.5 19.3 %collective-permute-start.7 = (bf16[768,512]{1,0:T(8,128)(2,1)S(1)}, bf16[768,512]{1,0:T(8,128)(2,1)}, u32[]{:S(2)}, u32[]{:S(2)}) collective-permute-start(bf16[768,512]{1,0:T(8,128)(2,1)S(1)} %collective-permute-done.refs_8_.refs_12_.refs_9_.refs_13_), channel_id=1, source_target_pairs={{0,4},{1,5},{2,6},{3,7},{4,8},{5,9},{6,10},{7,11},{8,12},{9,13},{1... | collective-permute-start | bytes 2359304 | tf_op jit(solution)/shard_map/ppermute | solution.py:83
  54.8 28.9 %collective-permute-start.5 = (bf16[512,1024]{1,0:T(8,128)(2,1)S(1)}, bf16[512,1024]{1,0:T(8,128)(2,1)}, u32[]{:S(2)}, u32[]{:S(2)}) collective-permute-start(bf16[512,1024]{1,0:T(8,128)(2,1)S(1)} %collective-permute-done.1), channel_id=1, source_target_pairs={{0,2},{1,3},{2,128},{3,129},{4,6},{5,7},{6,132},{7,133},{8,10},{9,... | collective-permute-start | bytes 3145736 | tf_op jit(solution)/shard_map/ppermute | solution.py:89
  58.1 16.9 %collective-permute-start.6 = (bf16[768,512]{1,0:T(8,128)(2,1)S(1)}, bf16[768,512]{1,0:T(8,128)(2,1)S(1)}, u32[]{:S(2)}, u32[]{:S(2)}) collective-permute-start(bf16[768,512]{1,0:T(8,128)(2,1)S(1)} %collective-permute-done.refs_8_.refs_12_.refs_9_.refs_13_), channel_id=1, source_target_pairs={{0,12},{1,13},{2,14},{3,15},{4,0},{5,1},{6,2},{7,3},{8,4},{9,5},{1... | collective-permute-start | bytes 2359304 | tf_op jit(solution)/shard_map/ppermute | solution.py:86
  72.9 12.3 %collective-permute-start.8 = (bf16[768,512]{1,0:T(8,128)(2,1)}, bf16[768,512]{1,0:T(8,128)(2,1)}, u32[]{:S(2)}, u32[]{:S(2)}) collective-permute-start(bf16[768,512]{1,0:T(8,128)(2,1)} %collective-permute-done.7.refs_9_.refs_13_.refs_10_.refs_14_), channel_id=1, source_target_pairs={{0,4},{1,5},{2,6},{3,7},{4,8},{5,9},{6,10},{7,11},{8,12},{9,13},{1... | collective-permute-start | bytes 2359304 | tf_op jit(solution)/shard_map/ppermute | solution.py:83
  75.0 0.9 copy-start.7
  85.2 16.7 %collective-permute-start.9 = (bf16[768,512]{1,0:T(8,128)(2,1)}, bf16[768,512]{1,0:T(8,128)(2,1)}, u32[]{:S(2)}, u32[]{:S(2)}) collective-permute-start(bf16[768,512]{1,0:T(8,128)(2,1)} %refs_5_), channel_id=1, source_target_pairs={{0,3},{1,0},{2,1},{3,2},{4,7},{5,4},{6,5},{7,6},{8,11},{9,8},{10,9... | collective-permute-start | bytes 2359304 | tf_op jit(solution)/shard_map/ppermute | solution.py:92
  101.9 18.8 %collective-permute-start.10 = (bf16[768,512]{1,0:T(8,128)(2,1)}, bf16[768,512]{1,0:T(8,128)(2,1)}, u32[]{:S(2)}, u32[]{:S(2)}) collective-permute-start(bf16[768,512]{1,0:T(8,128)(2,1)} %collective-permute-done.9.refs_17_), channel_id=1, source_target_pairs={{0,4},{1,5},{2,6},{3,7},{4,8},{5,9},{6,10},{7,11},{8,12},{9,13},{1... | collective-permute-start | bytes 2359304 | tf_op jit(solution)/shard_map/ppermute | solution.py:83
  102.8 17.9 %collective-permute-start.11 = (bf16[768,512]{1,0:T(8,128)(2,1)}, bf16[768,512]{1,0:T(8,128)(2,1)}, u32[]{:S(2)}, u32[]{:S(2)}) collective-permute-start(bf16[768,512]{1,0:T(8,128)(2,1)} %collective-permute-done.9.refs_17_), channel_id=1, source_target_pairs={{0,12},{1,13},{2,14},{3,15},{4,0},{5,1},{6,2},{7,3},{8,4},{9,5},{1... | collective-permute-start | bytes 2359304 | tf_op jit(solution)/shard_map/ppermute | solution.py:86
  104.0 16.6 %collective-permute-start.12 = (bf16[768,512]{1,0:T(8,128)(2,1)S(1)}, bf16[768,512]{1,0:T(8,128)(2,1)}, u32[]{:S(2)}, u32[]{:S(2)}) collective-permute-start(bf16[768,512]{1,0:T(8,128)(2,1)S(1)} %collective-permute-done.refs_8_.refs_12_.refs_9_.refs_13_), channel_id=1, source_target_pairs={{0,1},{1,2},{2,3},{3,0},{4,5},{5,6},{6,7},{7,4},{8,9},{9,10},{10,1... | collective-permute-start | bytes 2359304 | tf_op jit(solution)/shard_map/ppermute | solution.py:92
  105.9 37.5 %copy-start.10 = (s32[192]{0:T(256)S(1)}, s32[192]{0:T(256)}, u32[]{:S(2)}) copy-start(s32[192]{0:T(256)} %param.9) | copy-start | bytes 2308
  120.7 19.8 %collective-permute-start.13 = (bf16[768,512]{1,0:T(8,128)(2,1)}, bf16[768,512]{1,0:T(8,128)(2,1)S(1)}, u32[]{:S(2)}, u32[]{:S(2)}) collective-permute-start(bf16[768,512]{1,0:T(8,128)(2,1)} %collective-permute-done.11.refs_19_), channel_id=1, source_target_pairs={{0,12},{1,13},{2,14},{3,15},{4,0},{5,1},{6,2},{7,3},{8,4},{9,5},{1... | collective-permute-start | bytes 2359304 | tf_op jit(solution)/shard_map/ppermute | solution.py:86
  124.0 16.5 %collective-permute-start.14 = (bf16[768,512]{1,0:T(8,128)(2,1)}, bf16[768,512]{1,0:T(8,128)(2,1)S(1)}, u32[]{:S(2)}, u32[]{:S(2)}) collective-permute-start(bf16[768,512]{1,0:T(8,128)(2,1)} %collective-permute-done.12.refs_21_), channel_id=1, source_target_pairs={{0,4},{1,5},{2,6},{3,7},{4,8},{5,9},{6,10},{7,11},{8,12},{9,13},{1... | collective-permute-start | bytes 2359304 | tf_op jit(solution)/shard_map/ppermute | solution.py:83
  140.5 0.9 copy-start.9
  141.4 2.3 %copy-start.8 = (bf16[768,512]{1,0:T(8,128)(2,1)}, bf16[768,512]{1,0:T(8,128)(2,1)S(1)}, u32[]{:S(2)}) copy-start(bf16[768,512]{1,0:T(8,128)(2,1)S(1)} %collective-permute-done.14.refs_22_) | copy-start | bytes 2359300
  141.4 18.3 %collective-permute-start.15 = (bf16[768,512]{1,0:T(8,128)(2,1)}, bf16[768,512]{1,0:T(8,128)(2,1)S(1)}, u32[]{:S(2)}, u32[]{:S(2)}) collective-permute-start(bf16[768,512]{1,0:T(8,128)(2,1)} %collective-permute-done.12.refs_21_), channel_id=1, source_target_pairs={{0,12},{1,13},{2,14},{3,15},{4,0},{5,1},{6,2},{7,3},{8,4},{9,5},{1... | collective-permute-start | bytes 2359304 | tf_op jit(solution)/shard_map/ppermute | solution.py:86
  142.4 17.3 %collective-permute-start.16 = (bf16[768,512]{1,0:T(8,128)(2,1)S(1)}, bf16[768,512]{1,0:T(8,128)(2,1)S(1)}, u32[]{:S(2)}, u32[]{:S(2)}) collective-permute-start(bf16[768,512]{1,0:T(8,128)(2,1)S(1)} %collective-permute-done.14.refs_22_), channel_id=1, source_target_pairs={{0,4},{1,5},{2,6},{3,7},{4,8},{5,9},{6,10},{7,11},{8,12},{9,13},{1... | collective-permute-start | bytes 2359304 | tf_op jit(solution)/shard_map/ppermute | solution.py:83
  143.7 16.1 %copy-start = (bf16[768,1024]{1,0:T(8,128)(2,1)S(1)}, bf16[768,1024]{1,0:T(8,128)(2,1)}, u32[]{:S(2)}) copy-start(bf16[768,1024]{1,0:T(8,128)(2,1)} %student_ref.1) | copy-start | bytes 4718596
  143.7 16.0 %copy-start.1 = (f32[8192]{0:T(1024)S(1)}, f32[8192]{0:T(1024)}, u32[]{:S(2)}) copy-start(f32[8192]{0:T(1024)} %param.6) | copy-start | bytes 98308
  143.7 16.0 %copy-start.2 = (s32[48]{0:T(128)S(1)}, s32[48]{0:T(128)}, u32[]{:S(2)}) copy-start(s32[48]{0:T(128)} %stack.151.plan_ref) | copy-start | bytes 580
  165.8 5.1 %collective-permute-start.17 = (f32[8,768]{1,0:T(8,128)S(1)}, f32[8,768]{1,0:T(8,128)S(1)}, u32[]{:S(2)}, u32[]{:S(2)}) collective-permute-start(f32[8,768]{1,0:T(8,128)S(1)} %get-tuple-element.32.own_ref), channel_id=1, source_target_pairs={{0,1},{1,0},{2,3},{3,2},{4,5},{5,4},{6,7},{7,6},{8,9},{9,8},{10,11... | collective-permute-start | bytes 73736 | tf_op jit(solution)/shard_map/ppermute | solution.py:391
  165.9 5.0 %collective-permute-start.18 = (f32[8,768]{1,0:T(8,128)S(1)}, f32[8,768]{1,0:T(8,128)S(1)}, u32[]{:S(2)}, u32[]{:S(2)}) collective-permute-start(f32[8,768]{1,0:T(8,128)S(1)} %get-tuple-element.32.own_ref), channel_id=1, source_target_pairs={{0,2},{1,3},{2,0},{3,1},{4,6},{5,7},{6,4},{7,5},{8,10},{9,11},{10,... | collective-permute-start | bytes 73736 | tf_op jit(solution)/shard_map/ppermute | solution.py:391
  166.1 6.2 %collective-permute-start.19 = (f32[8,768]{1,0:T(8,128)S(1)}, f32[8,768]{1,0:T(8,128)S(1)}, u32[]{:S(2)}, u32[]{:S(2)}) collective-permute-start(f32[8,768]{1,0:T(8,128)S(1)} %get-tuple-element.32.own_ref), channel_id=1, source_target_pairs={{0,3},{1,2},{2,1},{3,0},{4,7},{5,6},{6,5},{7,4},{8,11},{9,10},{10,... | collective-permute-start | bytes 73736 | tf_op jit(solution)/shard_map/ppermute | solution.py:391
  173.0 1.1 collective-permute-start.20
  174.2 10.9 %collective-permute-start.21 = (f32[1,128]{1,0:T(1,128)S(1)}, f32[1,128]{1,0:T(1,128)S(1)}, u32[]{:S(2)}, u32[]{:S(2)}) collective-permute-start(f32[1,128]{1,0:T(1,128)S(1)} %add.374), channel_id=1, source_target_pairs={{0,128},{16,144},{32,160},{48,176},{64,192},{80,208},{96,224},{112... | collective-permute-start | bytes 1544 | tf_op jit(solution)/shard_map/ppermute | solution.py:380
  185.1 5.3 %collective-permute-start.22 = (f32[1,128]{1,0:T(1,128)S(1)}, f32[1,128]{1,0:T(1,128)S(1)}, u32[]{:S(2)}, u32[]{:S(2)}) collective-permute-start(f32[1,128]{1,0:T(1,128)S(1)} %add.375), channel_id=1, source_target_pairs={{0,32},{16,48},{32,64},{48,80},{64,96},{80,112},{96,0},{112,16},{1... | collective-permute-start | bytes 1544 | tf_op jit(solution)/shard_map/ppermute | solution.py:380
  186.1 5.0 %collective-permute-start.23 = (f32[1,128]{1,0:T(1,128)S(1)}, f32[1,128]{1,0:T(1,128)S(1)}, u32[]{:S(2)}, u32[]{:S(2)}) collective-permute-start(f32[1,128]{1,0:T(1,128)S(1)} %add.375), channel_id=1, source_target_pairs={{0,64},{16,80},{32,96},{48,112},{64,0},{80,16},{96,32},{112,48},{1... | collective-permute-start | bytes 1544 | tf_op jit(solution)/shard_map/ppermute | solution.py:380
  189.6 3.5 %collective-permute-start.24 = (f32[1,128]{1,0:T(1,128)S(1)}, f32[1,128]{1,0:T(1,128)S(1)}, u32[]{:S(2)}, u32[]{:S(2)}) collective-permute-start(f32[1,128]{1,0:T(1,128)S(1)} %add.375), channel_id=1, source_target_pairs={{0,96},{16,112},{32,0},{48,16},{64,32},{80,48},{96,64},{112,80},{1... | collective-permute-start | bytes 1544 | tf_op jit(solution)/shard_map/ppermute | solution.py:380
  193.1 7.2 %collective-permute-start.25 = (f32[1,128]{1,0:T(1,128)S(1)}, f32[1,128]{1,0:T(1,128)S(1)}, u32[]{:S(2)}, u32[]{:S(2)}) collective-permute-start(f32[1,128]{1,0:T(1,128)S(1)} %add_add_fusion.1), channel_id=1, source_target_pairs={{0,4},{1,5},{2,6},{3,7},{4,8},{5,9},{6,10},{7,11},{8,12},{9,13},{1... | collective-permute-start | bytes 1544 | tf_op jit(solution)/shard_map/ppermute | solution.py:380
  195.0 5.3 %collective-permute-start.26 = (f32[1,128]{1,0:T(1,128)S(1)}, f32[1,128]{1,0:T(1,128)S(1)}, u32[]{:S(2)}, u32[]{:S(2)}) collective-permute-start(f32[1,128]{1,0:T(1,128)S(1)} %add_add_fusion.1), channel_id=1, source_target_pairs={{0,8},{1,9},{2,10},{3,11},{4,12},{5,13},{6,14},{7,15},{8,0},{9,1},... | collective-permute-start | bytes 1544 | tf_op jit(solution)/shard_map/ppermute | solution.py:380
  197.8 3.8 %collective-permute-start.27 = (f32[1,128]{1,0:T(1,128)S(1)}, f32[1,128]{1,0:T(1,128)S(1)}, u32[]{:S(2)}, u32[]{:S(2)}) collective-permute-start(f32[1,128]{1,0:T(1,128)S(1)} %add_add_fusion.1), channel_id=1, source_target_pairs={{0,12},{1,13},{2,14},{3,15},{4,0},{5,1},{6,2},{7,3},{8,4},{9,5},{1... | collective-permute-start | bytes 1544 | tf_op jit(solution)/shard_map/ppermute | solution.py:380
Sparse Core Ops, SparseCore 0:
  9.9 55.2 all-gather.4
  85.3 54.4 all-gather.6
where the time goes:
time: 213 us; the launch traced here: 212 us
  waiting for transfers between devices  102 us (48%)
  starting transfers between devices  55 us (26%)
  Pallas kernels  33.4 us (16%)
  between operations  16.7 us (8%)
  local copies, waits for them, and re-layouts  3.35 us (2%)
    ppermute x3, waiting for transfers between devices, z_hop(): return lax.ppermute(value, 'tp', z_ring(d))  35.4 us
    pallas_call x3, Pallas kernels, accumulate_blocks(): pl.pallas_call(functools.partial(teacher_kernel, first, [len(block) for b...  30.1 us
    ppermute x7, waiting for transfers between devices, first(): return lax.ppermute(value, ('rows', 'tp'), whole(x_first))  29.7 us
    ppermute x5, waiting for transfers between devices, second(): return lax.ppermute(value, ('rows', 'tp'), whole(x_second))  22.3 us
    ppermute x8, starting transfers between devices, stage(): return sum([lax.ppermute(value, axis, move) for move in moves], value)  20.9 us
    ppermute x7, starting transfers between devices, first(): return lax.ppermute(value, ('rows', 'tp'), whole(x_first))  8.97 us
    ppermute x2, waiting for transfers between devices, far_hop(): return lax.ppermute(value, ('rows', 'tp'), whole(z_two))  7.77 us
    ppermute x3, starting transfers between devices, z_hop(): return lax.ppermute(value, 'tp', z_ring(d))  7.19 us
  transfers between devices with their start and end apart: 30, of which 14 were waited for; matrix products, arithmetic and copies ran while one was open for 1% of the time, Pallas kernels for 13%

commit v1 on v0

--- a/solution.py
+++ b/solution.py
@@ -16,7 +16,7 @@
 NY = 4
 NH = 2
 BLOCKS = 16
-CHUNK = 256
+CHUNK = 128
 MIB = 1 << 20
 
 
@@ -66,6 +66,18 @@
     return h, y, c, (x - way(c)) % NX, z
 
 
+def y_first(h, y, c, x, z):
+    return h, (y + way(c)) % NY, c, x, z
+
+
+def y_second(h, y, c, x, z):
+    return h, (y - way(c)) % NY, c, x, z
+
+
+def other_core(h, y, c, x, z):
+    return h, y, 1 - c, x, z
+
+
 def z_two(h, y, c, x, z):
     there = (h * NZ + z + 2 * way(c)) % (NH * NZ)
     return there // NZ, y, c, x, there % NZ
@@ -75,55 +87,67 @@
     return [(r, r ^ m) for r in range(16)]
 
 
-SAME_HALF = [[row_at(h, y, c) for y in range(NY) for c in range(2)] for h in range(NH)]
-
-
 def teacher_logits(weight, own, accumulate):
-    def first(value):
-        return lax.ppermute(value, ("rows", "tp"), whole(x_first))
-
-    def second(value):
-        return lax.ppermute(value, ("rows", "tp"), whole(x_second))
-
-    def far_hop(value):
-        return lax.ppermute(value, ("rows", "tp"), whole(z_two))
+    def go(move):
+        pairs = whole(move)
+        return lambda value: lax.ppermute(value, ("rows", "tp"), pairs)
+
+    first, second, far_hop = go(x_first), go(x_second), go(z_two)
+    y_one, y_two, swap = go(y_first), go(y_second), go(other_core)
 
     def z_hop(value, d):
         return lax.ppermute(value, "tp", z_ring(d))
 
-    def widen(shard):
-        return lax.all_gather(shard, "rows", axis_index_groups=SAME_HALF)
-
-    near = widen(weight)
     z1 = z_hop(own, 1)
     half_way = far_hop(weight)
     first0, second0 = first(own), second(own)
+    near1, near3 = y_one(weight), y_two(weight)
     third0 = first(first0)
 
-    here1, half_way, own, *_ = lax.optimization_barrier((z1, half_way, own, second0, third0))
+    other0 = swap(weight)
+
+    here1, half_way, own, near1, near3, *_ = lax.optimization_barrier(
+        (z1, half_way, own, near1, near3, second0, third0, other0)
+    )
     first1, second1 = first(here1), second(here1)
-    third1 = first(first1)
-    far = far_hop(half_way)
-
-    far, here1, own, *_ = lax.optimization_barrier((far, here1, own, second1, third1))
-    far = widen(far)
+    near2 = y_one(near1)
+    other1 = swap(near1)
+    far0 = far_hop(half_way)
+
+    far0, here1, own, on1, near2, near3, *_ = lax.optimization_barrier(
+        (far0, here1, own, first1, near2, near3, second1, other1)
+    )
     z3 = z_hop(own, -1)
-
-    here3, here1 = lax.optimization_barrier((z3, here1))
+    third1 = first(on1)
+    other2, other3, other4 = swap(near2), swap(near3), swap(far0)
+
+    here3, here1, far0, third1, *_ = lax.optimization_barrier(
+        (z3, here1, far0, third1, other2, other3, other4)
+    )
+    far1, far3 = y_one(far0), y_two(far0)
     z2 = z_hop(here1, 1)
     first3, second3 = first(here3), second(here3)
     groups = [[own, first0, third0, second0], [here1, first1, third1, second1]]
-    state = accumulate(0, [groups[0], groups[0], groups[1], groups[1]], near, near)
-
-    here2, on3, *_ = lax.optimization_barrier((z2, second3, first3, state))
+    blocks = [groups[0], groups[0], groups[1], groups[1]]
+    near = [weight, near1, near2, near3, other0, other1, other2, other3]
+    (state,) = accumulate(0, blocks, near)
+
+    here2, on3, far1, far3, *_ = lax.optimization_barrier(
+        (z2, second3, far1, far3, first3, state)
+    )
     first2, third3 = first(here2), second(on3)
-
-    here2, on2, *_ = lax.optimization_barrier((here2, first2, third3))
+    far2 = y_one(far1)
+    other5, other7 = swap(far1), swap(far3)
+
+    here2, on2, far2, *_ = lax.optimization_barrier(
+        (here2, first2, far2, third3, other5, other7)
+    )
     second2, third2 = second(here2), first(on2)
-    blocks = [groups[0], groups[0], groups[1], groups[1]]
+    other6 = swap(far2)
     blocks += [[one] for one in (here3, first3, second3, third3, here2, first2)]
-    state = accumulate(4, blocks, near, far, state)
-    return accumulate(14, [[second2], [third2]], near, far, state)
+    far = [far0, far1, far2, far3, other4, other5, other6, other7]
+    state, picked = accumulate(4, blocks, near + far, state)
+    return accumulate(14, [[second2], [third2]], [picked], state)
 
 
 ORDER = [(0, None), (0, None), (1, None), (1, None)] * 2
@@ -144,24 +168,28 @@
         block = ((x - off * turn) % NX) * NZ + (z - i) % NZ
         offsets.append(jnp.asarray(off, jnp.int32))
         blocks.append(block)
-        slots.append(jnp.where(block // 8 == half, block % 8, 8 + block % 8))
+        same = block % 2 == row % 2
+        y_off = ((row % 8 // 2 - block % 8 // 2) * jnp.where(same, turn, -turn)) % NY
+        slots.append(jnp.where(block // 8 == half, 0, 8) + jnp.where(same, 0, 4) + y_off)
     return jnp.stack(slots + blocks + offsets).astype(jnp.int32)
 
 
-def teacher_kernel(first, choices, plan_ref, gain_ref, near_ref, far_ref, *refs):
+def teacher_kernel(first, choices, n_weights, plan_ref, gain_ref, *refs):
     refs = list(refs)
     count = len(choices)
     last = first + count == BLOCKS
     student_ref = refs.pop(0) if last else None
     state_ref = refs.pop(0) if first else None
+    weights = [refs.pop(0) for _ in range(n_weights)]
     blocks = [[refs.pop(0) for _ in range(n)] for n in choices]
     out_ref = refs.pop(0)
     stats_ref = refs.pop(0) if last else None
-    total_ref, a_vm, w_vm, a_sem, w_sem, state_sem, *extra = refs
+    picked_ref = refs.pop(0) if first and not last else None
+    total_ref, a_vm, w_vm, a_sem, w_sem, state_sem, out_sem, *extra = refs
     tok, width = total_ref.shape
     cols = width - 128
 
-    def start(step):
+    def start_block(step):
         for off, block in enumerate(blocks[step]):
             wanted = plan_ref[2 * BLOCKS + first + step] == off if len(blocks[step]) > 1 else True
 
@@ -169,18 +197,33 @@
             def _():
                 pltpu.make_async_copy(block, a_vm.at[step], a_sem.at[step]).start()
 
+    def start_weights(step, carry=0):
+        to, sem = w_vm.at[step], w_sem.at[step]
+        if last:
+            pltpu.make_async_copy(weights[0].at[step], to, sem).start()
+            return carry
         slot = plan_ref[first + step]
-
-        @pl.when(slot < 8)
-        def _():
-            pltpu.make_async_copy(near_ref.at[slot], w_vm.at[step], w_sem.at[step]).start()
-
-        @pl.when(slot >= 8)
-        def _():
-            pltpu.make_async_copy(far_ref.at[slot - 8], w_vm.at[step], w_sem.at[step]).start()
-
-    def multiply(step, r, more=None):
-        rows = slice(r, r + CHUNK)
+        for at, ref in enumerate(weights):
+
+            @pl.when(slot == at)
+            def _():
+                pltpu.make_async_copy(ref, to, sem).start()
+
+        return carry
+
+    def each_chunk(do):
+        if picked_ref is not None:
+            for at in range(0, tok, 2 * CHUNK):
+                do(pl.ds(at, 2 * CHUNK))
+            return
+
+        def one(at, carry):
+            do(pl.ds(pl.multiple_of(at * CHUNK, CHUNK), CHUNK))
+            return carry
+
+        lax.fori_loop(0, tok // CHUNK, one, 0)
+
+    def multiply(step, rows, more=None):
         wide = a_vm[step, rows, :].astype(jnp.float32)
         square = wide * wide
         square = square[:, :128] + square[:, 128:256] + square[:, 256:384] + square[:, 384:]
@@ -189,7 +232,7 @@
         if more is not None:
             total += more[rows, :cols]
             square += more[rows, cols:]
-        return rows, total, square
+        return total, square
 
     def arrive(step):
         pltpu.make_async_copy(a_vm.at[step], a_vm.at[step], a_sem.at[step]).wait()
@@ -201,48 +244,88 @@
 
             @pl.when(step + 2 == later)
             def _():
-                start(later)
-
-        for r in range(0, tok, CHUNK):
-            rows, total, square = multiply(step, r, total_ref)
+                start_block(later)
+
+        @pl.when(step + 2 < count)
+        def _():
+            start_weights(step + 2)
+
+        if picked_ref is not None:
+
+            @pl.when((step == 2) | (step == 3))
+            def _():
+                start_weights(count + step - 2)
+
+            @pl.when(step == 6)
+            def _():
+                for at in range(2):
+                    pick = w_vm.at[count + at]
+                    sem = w_sem.at[count + at]
+                    pltpu.make_async_copy(pick, pick, sem).wait()
+                    pltpu.make_async_copy(pick, picked_ref.at[at], sem).start()
+
+        def add(rows):
+            total, square = multiply(step, rows, total_ref)
             total_ref[rows, :cols] = total
             total_ref[rows, cols:] = square
+
+        each_chunk(add)
         return carry
 
-    start(0)
+    start_block(0)
+    start_block(1)
+    lax.fori_loop(0, 2, start_weights, 0)
     if last:
         state_vm, stud_vm, stud_sem = extra
         student = pltpu.make_async_copy(student_ref, stud_vm, stud_sem)
         state = pltpu.make_async_copy(state_ref.at[pl.ds(0, tok)], state_vm, state_sem)
-        start(1)
         state.start()
         student.start()
         arrive(0)
-        for r in range(0, tok, CHUNK):
-            rows, total, square = multiply(0, r)
+
+        def begin(rows):
+            total, square = multiply(0, rows)
             total_ref[rows, :cols] = total
             total_ref[rows, cols:] = square
+
+        each_chunk(begin)
         arrive(1)
         state.wait()
         student.wait()
-        for r in range(0, tok, CHUNK):
-            rows, total, square = multiply(1, r, total_ref)
+
+        def finish(rows):
+            total, square = multiply(1, rows, total_ref)
             total += state_vm[rows, :cols]
             square += state_vm[rows, cols:]
             stats_ref[:, rows] = statistics(total, square, stud_vm[rows, :], out_ref, rows)
+
+        each_chunk(finish)
         return
     if first:
-        state = pltpu.make_async_copy(state_ref.at[pl.ds(0, tok)], total_ref, state_sem)
+        state = pltpu.make_async_copy(state_ref.at[pl.ds(0, tok)], extra[0], state_sem)
         state.start()
-        start(1)
+    total_ref[...] = jnp.zeros_like(total_ref)
+    lax.fori_loop(0, count, whole_step, 0)
+    if first:
         state.wait()
-    else:
-        start(1)
-        total_ref[...] = jnp.zeros_like(total_ref)
-    lax.fori_loop(0, count, whole_step, 0)
-    result = pltpu.make_async_copy(total_ref, out_ref.at[pl.ds(0, tok)], state_sem)
-    result.start()
-    result.wait()
+    copies = []
+    for r in range(0, tok, CHUNK):
+        rows = pl.ds(r, CHUNK)
+        if first:
+            total_ref[rows, :] += extra[0][rows, :]
+        copies.append(
+            pltpu.make_async_copy(total_ref.at[rows], out_ref.at[rows], out_sem.at[r // CHUNK])
+        )
+        copies[-1].start()
+    if picked_ref is not None:
+        for at in range(2):
+            copies.append(
+                pltpu.make_async_copy(
+                    w_vm.at[count + at], picked_ref.at[at], w_sem.at[count + at]
+                )
+            )
+    for copy in copies:
+        copy.wait()
 
 
 def statistics(logits, square, student, out_ref, rows):
@@ -265,41 +348,45 @@
     return packed.T[:8, :]
 
 
-def accumulate_blocks(gain, student, plan, first, blocks, near, far, state=None):
+def accumulate_blocks(gain, student, plan, first, blocks, weights, state=None):
     tok, cols = student.shape
     hbm = pl.BlockSpec(memory_space=pltpu.HBM)
     vmem = pl.BlockSpec(memory_space=pltpu.VMEM)
     smem = pl.BlockSpec(memory_space=pltpu.SMEM)
     anywhere = pl.BlockSpec(memory_space=pl.ANY)
     logits = jax.ShapeDtypeStruct((tok, cols), jnp.float32)
-    totals = jax.ShapeDtypeStruct((8 * tok, cols + 128), jnp.float32)
+    totals = jax.ShapeDtypeStruct(((8 if first else 1) * tok, cols + 128), jnp.float32)
+    picked = jax.ShapeDtypeStruct((24, 512, cols), jnp.bfloat16)
     stats = jax.ShapeDtypeStruct((8, tok), jnp.float32)
     count = len(blocks)
     last = first + count == BLOCKS
     scratch = [
         pltpu.VMEM((tok, cols + 128), jnp.float32),
         pltpu.VMEM((count, tok, 512), jnp.bfloat16),
-        pltpu.VMEM((count, 512, cols), jnp.bfloat16),
+        pltpu.VMEM((count + 2, 512, cols), jnp.bfloat16),
         pltpu.SemaphoreType.DMA((count,)),
-        pltpu.SemaphoreType.DMA((count,)),
+        pltpu.SemaphoreType.DMA((count + 2,)),
         pltpu.SemaphoreType.DMA,
+        pltpu.SemaphoreType.DMA((tok // CHUNK,)),
     ]
+    if first:
+        scratch += [pltpu.VMEM((tok, cols + 128), jnp.float32)]
     if last:
         scratch += [
-            pltpu.VMEM((tok, cols + 128), jnp.float32),
             pltpu.VMEM((tok, cols), jnp.bfloat16),
             pltpu.SemaphoreType.DMA,
         ]
-    parts = [student] * last + [state] * (first > 0) + [one for block in blocks for one in block]
+    parts = [student] * last + [state] * (first > 0) + weights
+    parts += [one for block in blocks for one in block]
     return pl.pallas_call(
-        functools.partial(teacher_kernel, first, [len(block) for block in blocks]),
-        out_shape=(logits, stats) if last else totals,
-        in_specs=[smem, vmem] + [hbm] * 2 + [anywhere] * len(parts),
-        out_specs=(vmem, vmem) if last else hbm,
+        functools.partial(teacher_kernel, first, [len(block) for block in blocks], len(weights)),
+        out_shape=(logits, stats) if last else (totals, picked) if first else (totals,),
+        in_specs=[smem, vmem] + [anywhere] * len(parts),
+        out_specs=(vmem, vmem) if last else (hbm, hbm) if first else (hbm,),
         scratch_shapes=scratch,
         compiler_params=pltpu.CompilerParams(vmem_limit_bytes=(42 if last else 60) * MIB),
         name="teacher_" + str(first),
-    )(plan, gain.reshape(BLOCKS, 1, 512), near, far, *parts)
+    )(plan, gain.reshape(BLOCKS, 1, 512), *parts)
 
 
 def merge(first, second):
@@ -354,11 +441,16 @@
 
 
 def grad_kernel(coef_ref, teach_ref, student_ref, grad_ref):
-    coef = coef_ref[...].T
-    stud = student_ref[...].astype(jnp.float32)
-    prob = jnp.exp((stud - coef[:, 0:1]) - coef[:, 1:2])
-    differ = (stud - teach_ref[...]) - coef[:, 2:3]
-    grad_ref[...] = ((coef[:, 3:4] * prob) * differ).astype(jnp.bfloat16)
+    def one(at, carry):
+        rows = pl.ds(pl.multiple_of(at * CHUNK, CHUNK), CHUNK)
+        coef = coef_ref[:, rows].T
+        stud = student_ref[rows, :].astype(jnp.float32)
+        prob = jnp.exp((stud - coef[:, 0:1]) - coef[:, 1:2])
+        differ = (stud - teach_ref[rows, :]) - coef[:, 2:3]
+        grad_ref[rows, :] = ((coef[:, 3:4] * prob) * differ).astype(jnp.bfloat16)
+        return carry
+
+    lax.fori_loop(0, student_ref.shape[0] // CHUNK, one, 0)
 
 
 def gradient(coef, teach, student):

time: 213 us -> 217 us (1.019)
  waiting for transfers between devices: 102 us -> 117 us
  between operations: 16.7 us -> 5.34 us
  Pallas kernels: 33.4 us -> 38.6 us
  starting transfers between devices: 55 us -> 52.8 us
    ppermute x14 -> x28, waiting for transfers between devices: 59.8 us -> 73.2 us  [go(): return lambda value: lax.ppermute(value, ('rows', 'tp'), pairs)]
    ppermute x14 -> x28, starting transfers between devices: 22.4 us -> 30.4 us  [go(): return lambda value: lax.ppermute(value, ('rows', 'tp'), pairs)]
    ppermute x8, starting transfers between devices: 20.9 us -> 15.2 us  [stage(): return sum([lax.ppermute(value, axis, move) for move in moves], value)]
    pallas_call x3, Pallas kernels: 30.1 us -> 35.1 us  [accumulate_blocks(): pl.pallas_call(functools.partial(teacher_kernel, first, [len(block) for b...]
    ppermute x3, starting transfers between devices: 7.19 us -> 2.79 us  [z_hop(): return lax.ppermute(value, 'tp', z_ring(d))]
  transfers between devices with their start and end apart: 30 -> 42, of which waited for: 14 -> 23; matrix products, arithmetic and copies ran while one was open for 1% -> 1% of each run, Pallas kernels for 13% -> 14%
where the time goes in v1:
time: 217 us
  waiting for transfers between devices  117 us (54%)
  starting transfers between devices  52.8 us (24%)
  Pallas kernels  38.6 us (18%)
  between operations  5.34 us (2%)
    ppermute x28, waiting for transfers between devices, go(): return lambda value: lax.ppermute(value, ('rows', 'tp'), pairs)  73.2 us
    pallas_call x3, Pallas kernels, accumulate_blocks(): pl.pallas_call(functools.partial(teacher_kernel, first, [len(block) for b...  35.1 us
    ppermute x3, waiting for transfers between devices, z_hop(): return lax.ppermute(value, 'tp', z_ring(d))  34.1 us
    ppermute x28, starting transfers between devices, go(): return lambda value: lax.ppermute(value, ('rows', 'tp'), pairs)  30.4 us
    ppermute x8, starting transfers between devices, stage(): return sum([lax.ppermute(value, axis, move) for move in moves], value)  15.2 us
    ppermute x8, waiting for transfers between devices, stage(): return sum([lax.ppermute(value, axis, move) for move in moves], value)  6.75 us
    ppermute x3, starting transfers between devices, body(): lax.ppermute(stats, 'tp', [(t, t ^ m) for t in range(BLOCKS)])  4.47 us
  transfers between devices with their start and end apart: 42, of which 23 were waited for; matrix products, arithmetic and copies ran while one was open for 1% of the time, Pallas kernels for 14%

profile of v1, /device:TPU:2, one launch (start us, length us, event | category | flops | bytes accessed | tf_op | source)
XLA Modules:
  0.0 216.6 jit_solution(12627578165989298684)
XLA Ops:
  0.6 1.6 collective-permute-start.5
  2.2 0.9 collective-permute-start.4
  3.1 1.6 collective-permute-start
  4.7 3.3 %collective-permute-start.1 = (bf16[512,1024]{1,0:T(8,128)(2,1)}, bf16[512,1024]{1,0:T(8,128)(2,1)S(1)}, u32[]{:S(2)}, u32[]{:S(2)}) collective-permute-start(bf16[512,1024]{1,0:T(8,128)(2,1)} %refs_1_.1), channel_id=1, source_target_pairs={{0,2},{1,3},{2,128},{3,129},{4,6},{5,7},{6,132},{7,133},{8,10},{9,... | collective-permute-start | bytes 3145736 | tf_op jit(solution)/shard_map/ppermute | solution.py:93
  7.9 13.6 %collective-permute-done.5.refs_9_.refs_13_.refs_18_.refs_22_ = bf16[768,512]{1,0:T(8,128)(2,1)S(1)} collective-permute-done((bf16[768,512]{1,0:T(8,128)(2,1)}, bf16[768,512]{1,0:T(8,128)(2,1)S(1)}, u32[]{:S(2)}, u32[]{:S(2)}) %collective-permute-start.5) | collective-permute-done | bytes 786464 | tf_op jit(solution)/shard_map/ppermute | solution.py:93
  21.5 1.2 collective-permute-start.2
  22.7 2.0 collective-permute-start.3
  24.7 12.6 %collective-permute-done.refs_16_.refs_20_.refs_25_.refs_29_ = bf16[768,512]{1,0:T(8,128)(2,1)S(1)} collective-permute-done((bf16[768,512]{1,0:T(8,128)(2,1)}, bf16[768,512]{1,0:T(8,128)(2,1)S(1)}, u32[]{:S(2)}, u32[]{:S(2)}) %collective-permute-start) | collective-permute-done | bytes 786464 | tf_op jit(solution)/shard_map/ppermute | solution.py:99
  37.3 1.5 collective-permute-start.6
  38.8 10.6 %collective-permute-done.1 = bf16[512,1024]{1,0:T(8,128)(2,1)S(1)} collective-permute-done((bf16[512,1024]{1,0:T(8,128)(2,1)}, bf16[512,1024]{1,0:T(8,128)(2,1)S(1)}, u32[]{:S(2)}, u32[]{:S(2)}) %collective-permute-start.1) | collective-permute-done | bytes 1048608 | tf_op jit(solution)/shard_map/ppermute | solution.py:93
  49.4 0.5 collective-permute-done.6.refs_10_.refs_14_.refs_19_.refs_23_
  50.0 1.3 collective-permute-start.10
  51.2 0.6 collective-permute-start.8
  51.8 2.1 collective-permute-start.11
  53.9 14.9 %collective-permute-done.11.refs_19_.refs_23_.refs_28_.refs_32_ = bf16[768,512]{1,0:T(8,128)(2,1)S(1)} collective-permute-done((bf16[768,512]{1,0:T(8,128)(2,1)S(1)}, bf16[768,512]{1,0:T(8,128)(2,1)S(1)}, u32[]{:S(2)}, u32[]{:S(2)}) %collective-permute-start.11) | collective-permute-done | bytes 786464 | tf_op jit(solution)/shard_map/ppermute | solution.py:93
  68.7 4.3 %collective-permute-done.9.refs_17_.refs_21_.refs_26_.refs_30_ = bf16[768,512]{1,0:T(8,128)(2,1)S(1)} collective-permute-done((bf16[768,512]{1,0:T(8,128)(2,1)S(1)}, bf16[768,512]{1,0:T(8,128)(2,1)S(1)}, u32[]{:S(2)}, u32[]{:S(2)}) %collective-permute-start.9) | collective-permute-done | bytes 786464 | tf_op jit(solution)/shard_map/ppermute | solution.py:93
  73.0 6.6 %collective-permute-done.8.refs_9_ = bf16[512,1024]{1,0:T(8,128)(2,1)} collective-permute-done((bf16[512,1024]{1,0:T(8,128)(2,1)S(1)}, bf16[512,1024]{1,0:T(8,128)(2,1)}, u32[]{:S(2)}, u32[]{:S(2)}) %collective-permute-start.8) | collective-permute-done | bytes 1048608 | tf_op jit(solution)/shard_map/ppermute | solution.py:93
  79.6 0.5 collective-permute-start.14
  80.2 0.3 collective-permute-start.15
  80.5 1.3 collective-permute-start.16
  81.7 18.7 %collective-permute-done.15.refs_33_ = bf16[768,512]{1,0:T(8,128)(2,1)} collective-permute-done((bf16[768,512]{1,0:T(8,128)(2,1)}, bf16[768,512]{1,0:T(8,128)(2,1)}, u32[]{:S(2)}, u32[]{:S(2)}) %collective-permute-start.15) | collective-permute-done | bytes 786464 | tf_op jit(solution)/shard_map/ppermute | solution.py:99
  100.5 1.7 collective-permute-start.20
  102.1 1.7 collective-permute-start.21
  103.8 2.5 %collective-permute-start.19 = (bf16[768,512]{1,0:T(8,128)(2,1)}, bf16[768,512]{1,0:T(8,128)(2,1)}, u32[]{:S(2)}, u32[]{:S(2)}) collective-permute-start(bf16[768,512]{1,0:T(8,128)(2,1)} %collective-permute-done.15.refs_33_), channel_id=1, source_target_pairs={{0,12},{1,13},{2,14},{3,15},{4,0},{5,1},{6,2},{7,3},{8,4},{9,5},{1... | collective-permute-start | bytes 2359304 | tf_op jit(solution)/shard_map/ppermute | solution.py:93
  106.3 0.9 collective-permute-start.18
  109.3 0.6 stack.151.plan_ref
  110.0 12.0 %teacher_0.1.refs_0_ = f32[768,1152]{1,0:T(8,128)} custom-call(s32[48]{0:T(128)} %stack.151.plan_ref, f32[16,1,512]{2,1,0:T(1,128)} %bitcast.39, bf16[512,1024]{1,0:T(8,128)(2,1)} %refs_1_.1, bf16[512,1024]{1,0:T(8,128)(2,1)} %copy-done.11, bf16[512,1024]{1,0:T(8,128)(2,1)} %copy-done.14, bf16[512,1024]{1,0:T(8,128)(2,1)} %copy-done.12, ...), custom_call_target="tpu_custom_call" | custom-call | tf_op jit(solution)/shard_map/teacher_0/pallas_call | solution.py:381
  122.0 1.4 collective-permute-done.19.refs_35_
  123.4 2.9 %collective-permute-done.18.refs_37_ = bf16[768,512]{1,0:T(8,128)(2,1)} collective-permute-done((bf16[768,512]{1,0:T(8,128)(2,1)S(1)}, bf16[768,512]{1,0:T(8,128)(2,1)}, u32[]{:S(2)}, u32[]{:S(2)}) %collective-permute-start.18) | collective-permute-done | bytes 786464 | tf_op jit(solution)/shard_map/ppermute | solution.py:99
  126.2 1.7 collective-permute-done.20.refs_10_
  128.0 0.3 collective-permute-start.26
  128.2 0.2 collective-permute-start.27
  128.5 1.0 collective-permute-start.23
  129.4 2.4 %collective-permute-start.25 = (bf16[768,512]{1,0:T(8,128)(2,1)}, bf16[768,512]{1,0:T(8,128)(2,1)S(1)}, u32[]{:S(2)}, u32[]{:S(2)}) collective-permute-start(bf16[768,512]{1,0:T(8,128)(2,1)} %collective-permute-done.19.refs_35_), channel_id=1, source_target_pairs={{0,12},{1,13},{2,14},{3,15},{4,0},{5,1},{6,2},{7,3},{8,4},{9,5},{1... | collective-permute-start | bytes 2359304 | tf_op jit(solution)/shard_map/ppermute | solution.py:93
  131.8 17.3 %collective-permute-done.23.refs_38_ = bf16[768,512]{1,0:T(8,128)(2,1)S(1)} collective-permute-done((bf16[768,512]{1,0:T(8,128)(2,1)}, bf16[768,512]{1,0:T(8,128)(2,1)S(1)}, u32[]{:S(2)}, u32[]{:S(2)}) %collective-permute-start.23) | collective-permute-done | bytes 786464 | tf_op jit(solution)/shard_map/ppermute | solution.py:93
  149.1 0.5 collective-permute-done.25.refs_36_
  149.7 0.7 collective-permute-start.28
  150.4 0.2 copy-done.18
  150.6 3.8 %collective-permute-start.29 = (bf16[768,512]{1,0:T(8,128)(2,1)}, bf16[768,512]{1,0:T(8,128)(2,1)S(1)}, u32[]{:S(2)}, u32[]{:S(2)}) collective-permute-start(bf16[768,512]{1,0:T(8,128)(2,1)} %collective-permute-done.18.refs_37_), channel_id=1, source_target_pairs={{0,12},{1,13},{2,14},{3,15},{4,0},{5,1},{6,2},{7,3},{8,4},{9,5},{1... | collective-permute-start | bytes 2359304 | tf_op jit(solution)/shard_map/ppermute | solution.py:93
  154.7 15.5 %teacher_4.1 = (f32[6144,1152]{1,0:T(8,128)}, bf16[24,512,1024]{2,1,0:T(8,128)(2,1)}) custom-call(s32[48]{0:T(128)} %stack.151.plan_ref, f32[16,1,512]{2,1,0:T(1,128)} %bitcast.40, f32[768,1152]{1,0:T(8,128)} %teacher_0.1.refs_0_, bf16[512,1024]{1,0:T(8,128)(2,1)} %refs_1_.1, bf16[512,1024]{1,0:T(8,128)(2,1)} %copy-done.11, bf16[512,1024]{1,0:T(8,128)(2,1)} %copy-done.14, ...), custom_call_target="tpu_custom_call" | custom-call | tf_op jit(solution)/shard_map/teacher_4/pallas_call | solution.py:381
  170.2 1.6 collective-permute-done.29.refs_3_
  171.8 0.3 collective-permute-done.30.refs_4_
  172.0 7.7 %teacher_14.1 = (f32[768,1024]{1,0:T(8,128)S(1)}, f32[8,768]{1,0:T(8,128)S(1)}) custom-call(s32[48]{0:T(128)S(1)} %copy-done.2, f32[16,1,512]{2,1,0:T(1,128)S(1)} %bitcast.41, bf16[768,1024]{1,0:T(8,128)(2,1)S(1)} %copy-done, f32[6144,1152]{1,0:T(8,128)} %get-tuple-element.53.refs_1_, bf16[24,512,1024]{2,1,0:T(8,128)(2,1)} %get-tuple-element.54.refs_2_, ...), custom_call_target="tpu_custom_call" | custom-call | tf_op jit(solution)/shard_map/teacher_14/pallas_call | solution.py:381
  179.7 0.5 collective-permute-start.31
  180.2 2.3 %collective-permute-start.32 = (f32[8,768]{1,0:T(8,128)S(1)}, f32[8,768]{1,0:T(8,128)S(1)}, u32[]{:S(2)}, u32[]{:S(2)}) collective-permute-start(f32[8,768]{1,0:T(8,128)S(1)} %get-tuple-element.56.own_ref), channel_id=1, source_target_pairs={{0,2},{1,3},{2,0},{3,1},{4,6},{5,7},{6,4},{7,5},{8,10},{9,11},{10,... | collective-permute-start | bytes 73736 | tf_op jit(solution)/shard_map/ppermute | solution.py:483
  182.5 1.7 collective-permute-start.33
  184.2 0.6 convert_reduce_fusion
  184.9 3.2 %collective-permute-done.33.fourth_ref = f32[8,768]{1,0:T(8,128)S(1)} collective-permute-done((f32[8,768]{1,0:T(8,128)S(1)}, f32[8,768]{1,0:T(8,128)S(1)}, u32[]{:S(2)}, u32[]{:S(2)}) %collective-permute-start.33) | collective-permute-done | bytes 24608 | tf_op jit(solution)/shard_map/ppermute | solution.py:483
  188.1 0.8 combine.1
  188.9 1.1 collective-permute-done.34
  190.0 4.1 %collective-permute-start.35 = (f32[1,128]{1,0:T(1,128)S(1)}, f32[1,128]{1,0:T(1,128)S(1)}, u32[]{:S(2)}, u32[]{:S(2)}) collective-permute-start(f32[1,128]{1,0:T(1,128)S(1)} %add.602), channel_id=1, source_target_pairs={{0,128},{16,144},{32,160},{48,176},{64,192},{80,208},{96,224},{112... | collective-permute-start | bytes 1544 | tf_op jit(solution)/shard_map/ppermute | solution.py:472
  194.1 2.7 %gradient.1 = bf16[768,1024]{1,0:T(8,128)(2,1)} custom-call(f32[8,768]{1,0:T(8,128)S(1)} %get-tuple-element.58.coef_ref, f32[768,1024]{1,0:T(8,128)S(1)} %get-tuple-element.59.teach_ref, bf16[768,1024]{1,0:T(8,128)(2,1)S(1)} %copy-done), custom_call_target="tpu_custom_call" | custom-call | tf_op jit(solution)/shard_map/gradient/pallas_call | solution.py:460
  196.8 0.6 collective-permute-done.35
  197.4 0.9 collective-permute-start.36
  198.3 3.1 %collective-permute-start.37 = (f32[1,128]{1,0:T(1,128)S(1)}, f32[1,128]{1,0:T(1,128)S(1)}, u32[]{:S(2)}, u32[]{:S(2)}) collective-permute-start(f32[1,128]{1,0:T(1,128)S(1)} %add.603), channel_id=1, source_target_pairs={{0,64},{16,80},{32,96},{48,112},{64,0},{80,16},{96,32},{112,48},{1... | collective-permute-start | bytes 1544 | tf_op jit(solution)/shard_map/ppermute | solution.py:472
  201.5 0.7 collective-permute-start.38
  202.2 1.2 collective-permute-done.37
  203.4 1.6 collective-permute-done.38
  205.0 1.3 collective-permute-start.39
  206.3 3.7 %collective-permute-start.40 = (f32[1,128]{1,0:T(1,128)S(1)}, f32[1,128]{1,0:T(1,128)S(1)}, u32[]{:S(2)}, u32[]{:S(2)}) collective-permute-start(f32[1,128]{1,0:T(1,128)S(1)} %add_add_fusion.1), channel_id=1, source_target_pairs={{0,8},{1,9},{2,10},{3,11},{4,12},{5,13},{6,14},{7,15},{8,0},{9,1},... | collective-permute-start | bytes 1544 | tf_op jit(solution)/shard_map/ppermute | solution.py:472
  210.0 1.3 collective-permute-start.41
  211.4 0.2 collective-permute-done.40
  211.5 2.0 collective-permute-done.41
  213.6 0.6 fusion
  (81 shorter events, 0.5 us)
Async XLA Ops:
  0.6 20.9 %collective-permute-start.5 = (bf16[768,512]{1,0:T(8,128)(2,1)}, bf16[768,512]{1,0:T(8,128)(2,1)S(1)}, u32[]{:S(2)}, u32[]{:S(2)}) collective-permute-start(bf16[768,512]{1,0:T(8,128)(2,1)} %refs_21_), channel_id=1, source_target_pairs={{0,4},{1,5},{2,6},{3,7},{4,8},{5,9},{6,10},{7,11},{8,12},{9,13},{1... | collective-permute-start | bytes 2359304 | tf_op jit(solution)/shard_map/ppermute | solution.py:93
  2.2 20.5 %collective-permute-start.4 = (bf16[768,512]{1,0:T(8,128)(2,1)}, bf16[768,512]{1,0:T(8,128)(2,1)S(1)}, u32[]{:S(2)}, u32[]{:S(2)}) collective-permute-start(bf16[768,512]{1,0:T(8,128)(2,1)} %refs_21_), channel_id=1, source_target_pairs={{0,12},{1,13},{2,14},{3,15},{4,0},{5,1},{6,2},{7,3},{8,4},{9,5},{1... | collective-permute-start | bytes 2359304 | tf_op jit(solution)/shard_map/ppermute | solution.py:93
  3.1 34.3 %collective-permute-start = (bf16[768,512]{1,0:T(8,128)(2,1)}, bf16[768,512]{1,0:T(8,128)(2,1)S(1)}, u32[]{:S(2)}, u32[]{:S(2)}) collective-permute-start(bf16[768,512]{1,0:T(8,128)(2,1)} %refs_21_), channel_id=1, source_target_pairs={{0,1},{1,2},{2,3},{3,0},{4,5},{5,6},{6,7},{7,4},{8,9},{9,10},{10,1... | collective-permute-start | bytes 2359304 | tf_op jit(solution)/shard_map/ppermute | solution.py:99
  4.7 34.2 %collective-permute-start.7 = (bf16[512,1024]{1,0:T(8,128)(2,1)}, bf16[512,1024]{1,0:T(8,128)(2,1)S(1)}, u32[]{:S(2)}, u32[]{:S(2)}) collective-permute-start(bf16[512,1024]{1,0:T(8,128)(2,1)} %refs_1_.1), channel_id=1, source_target_pairs={{0,16},{1,17},{2,18},{3,19},{4,20},{5,21},{6,22},{7,23},{8,24},{9,... | collective-permute-start | bytes 3145736 | tf_op jit(solution)/shard_map/ppermute | solution.py:93
  4.7 44.8 %collective-permute-start.1 = (bf16[512,1024]{1,0:T(8,128)(2,1)}, bf16[512,1024]{1,0:T(8,128)(2,1)S(1)}, u32[]{:S(2)}, u32[]{:S(2)}) collective-permute-start(bf16[512,1024]{1,0:T(8,128)(2,1)} %refs_1_.1), channel_id=1, source_target_pairs={{0,2},{1,3},{2,128},{3,129},{4,6},{5,7},{6,132},{7,133},{8,10},{9,... | collective-permute-start | bytes 3145736 | tf_op jit(solution)/shard_map/ppermute | solution.py:93
  21.5 88.4 %copy-start.3 = (bf16[768,512]{1,0:T(8,128)(2,1)}, bf16[768,512]{1,0:T(8,128)(2,1)S(1)}, u32[]{:S(2)}) copy-start(bf16[768,512]{1,0:T(8,128)(2,1)S(1)} %collective-permute-done.5.refs_9_.refs_13_.refs_18_.refs_22_) | copy-start | bytes 2359300
  21.5 27.9 %collective-permute-start.2 = (bf16[512,1024]{1,0:T(8,128)(2,1)}, bf16[512,1024]{1,0:T(8,128)(2,1)S(1)}, u32[]{:S(2)}, u32[]{:S(2)}) collective-permute-start(bf16[512,1024]{1,0:T(8,128)(2,1)} %refs_1_.1), channel_id=1, source_target_pairs={{0,32},{1,33},{2,34},{3,35},{4,36},{5,37},{6,38},{7,39},{8,40},{9,... | collective-permute-start | bytes 3145736 | tf_op jit(solution)/shard_map/ppermute | solution.py:93
  22.7 87.2 %copy-start.4 = (bf16[768,512]{1,0:T(8,128)(2,1)}, bf16[768,512]{1,0:T(8,128)(2,1)S(1)}, u32[]{:S(2)}) copy-start(bf16[768,512]{1,0:T(8,128)(2,1)S(1)} %collective-permute-done.4.refs_11_.refs_15_.refs_20_.refs_24_) | copy-start | bytes 2359300
  22.7 26.7 %collective-permute-start.3 = (bf16[512,1024]{1,0:T(8,128)(2,1)}, bf16[512,1024]{1,0:T(8,128)(2,1)S(1)}, u32[]{:S(2)}, u32[]{:S(2)}) collective-permute-start(bf16[512,1024]{1,0:T(8,128)(2,1)} %refs_1_.1), channel_id=1, source_target_pairs={{0,96},{1,97},{2,98},{3,99},{4,100},{5,101},{6,102},{7,103},{8,104... | collective-permute-start | bytes 3145736 | tf_op jit(solution)/shard_map/ppermute | solution.py:93
  37.3 72.6 %copy-start.5 = (bf16[768,512]{1,0:T(8,128)(2,1)}, bf16[768,512]{1,0:T(8,128)(2,1)S(1)}, u32[]{:S(2)}) copy-start(bf16[768,512]{1,0:T(8,128)(2,1)S(1)} %collective-permute-done.refs_16_.refs_20_.refs_25_.refs_29_) | copy-start | bytes 2359300
  37.3 12.6 %collective-permute-start.6 = (bf16[768,512]{1,0:T(8,128)(2,1)S(1)}, bf16[768,512]{1,0:T(8,128)(2,1)S(1)}, u32[]{:S(2)}, u32[]{:S(2)}) collective-permute-start(bf16[768,512]{1,0:T(8,128)(2,1)S(1)} %collective-permute-done.5.refs_9_.refs_13_.refs_18_.refs_22_), channel_id=1, source_target_pairs={{0,4},{1,5},{2,6},{3,7},{4,8},{5,9},{6,10},{7,11},{8,12},{9,13},{1... | collective-permute-start | bytes 2359304 | tf_op jit(solution)/shard_map/ppermute | solution.py:93
  38.8 12.4 %copy-start.10 = (bf16[512,1024]{1,0:T(8,128)(2,1)}, bf16[512,1024]{1,0:T(8,128)(2,1)S(1)}, u32[]{:S(2)}) copy-start(bf16[512,1024]{1,0:T(8,128)(2,1)S(1)} %collective-permute-done.7.refs_4_.refs_5_) | copy-start | bytes 3145732
  49.4 30.7 %copy-start.11 = (bf16[512,1024]{1,0:T(8,128)(2,1)}, bf16[512,1024]{1,0:T(8,128)(2,1)S(1)}, u32[]{:S(2)}) copy-start(bf16[512,1024]{1,0:T(8,128)(2,1)S(1)} %collective-permute-done.2.refs_1_.refs_2_) | copy-start | bytes 3145732
  49.4 57.8 %copy-start.12 = (bf16[512,1024]{1,0:T(8,128)(2,1)}, bf16[512,1024]{1,0:T(8,128)(2,1)S(1)}, u32[]{:S(2)}) copy-start(bf16[512,1024]{1,0:T(8,128)(2,1)S(1)} %collective-permute-done.3.refs_3_.refs_4_) | copy-start | bytes 3145732
  50.0 60.0 %copy-start.6 = (bf16[768,512]{1,0:T(8,128)(2,1)}, bf16[768,512]{1,0:T(8,128)(2,1)S(1)}, u32[]{:S(2)}) copy-start(bf16[768,512]{1,0:T(8,128)(2,1)S(1)} %collective-permute-done.6.refs_10_.refs_14_.refs_19_.refs_23_) | copy-start | bytes 2359300
  50.0 23.0 %collective-permute-start.12 = (bf16[512,1024]{1,0:T(8,128)(2,1)S(1)}, bf16[512,1024]{1,0:T(8,128)(2,1)S(1)}, u32[]{:S(2)}, u32[]{:S(2)}) collective-permute-start(bf16[512,1024]{1,0:T(8,128)(2,1)S(1)} %collective-permute-done.2.refs_1_.refs_2_), channel_id=1, source_target_pairs={{0,16},{1,17},{2,18},{3,19},{4,20},{5,21},{6,22},{7,23},{8,24},{9,... | collective-permute-start | bytes 3145736 | tf_op jit(solution)/shard_map/ppermute | solution.py:93
  50.0 23.1 %collective-permute-start.10 = (bf16[512,1024]{1,0:T(8,128)(2,1)S(1)}, bf16[512,1024]{1,0:T(8,128)(2,1)S(1)}, u32[]{:S(2)}, u32[]{:S(2)}) collective-permute-start(bf16[512,1024]{1,0:T(8,128)(2,1)S(1)} %collective-permute-done.2.refs_1_.refs_2_), channel_id=1, source_target_pairs={{0,32},{1,33},{2,34},{3,35},{4,36},{5,37},{6,38},{7,39},{8,40},{9,... | collective-permute-start | bytes 3145736 | tf_op jit(solution)/shard_map/ppermute | solution.py:93
  51.2 28.4 %collective-permute-start.8 = (bf16[512,1024]{1,0:T(8,128)(2,1)S(1)}, bf16[512,1024]{1,0:T(8,128)(2,1)}, u32[]{:S(2)}, u32[]{:S(2)}) collective-permute-start(bf16[512,1024]{1,0:T(8,128)(2,1)S(1)} %collective-permute-done.1), channel_id=1, source_target_pairs={{0,2},{1,3},{2,128},{3,129},{4,6},{5,7},{6,132},{7,133},{8,10},{9,... | collective-permute-start | bytes 3145736 | tf_op jit(solution)/shard_map/ppermute | solution.py:93
  51.8 17.0 %collective-permute-start.11 = (bf16[768,512]{1,0:T(8,128)(2,1)S(1)}, bf16[768,512]{1,0:T(8,128)(2,1)S(1)}, u32[]{:S(2)}, u32[]{:S(2)}) collective-permute-start(bf16[768,512]{1,0:T(8,128)(2,1)S(1)} %collective-permute-done.refs_16_.refs_20_.refs_25_.refs_29_), channel_id=1, source_target_pairs={{0,12},{1,13},{2,14},{3,15},{4,0},{5,1},{6,2},{7,3},{8,4},{9,5},{1... | collective-permute-start | bytes 2359304 | tf_op jit(solution)/shard_map/ppermute | solution.py:93
  53.9 19.1 %collective-permute-start.9 = (bf16[768,512]{1,0:T(8,128)(2,1)S(1)}, bf16[768,512]{1,0:T(8,128)(2,1)S(1)}, u32[]{:S(2)}, u32[]{:S(2)}) collective-permute-start(bf16[768,512]{1,0:T(8,128)(2,1)S(1)} %collective-permute-done.refs_16_.refs_20_.refs_25_.refs_29_), channel_id=1, source_target_pairs={{0,4},{1,5},{2,6},{3,7},{4,8},{5,9},{6,10},{7,11},{8,12},{9,13},{1... | collective-permute-start | bytes 2359304 | tf_op jit(solution)/shard_map/ppermute | solution.py:93
  68.7 37.6 %copy-start.7 = (bf16[768,512]{1,0:T(8,128)(2,1)}, bf16[768,512]{1,0:T(8,128)(2,1)S(1)}, u32[]{:S(2)}) copy-start(bf16[768,512]{1,0:T(8,128)(2,1)S(1)} %collective-permute-done.11.refs_19_.refs_23_.refs_28_.refs_32_) | copy-start | bytes 2359300
  73.0 33.3 %copy-start.8 = (bf16[768,512]{1,0:T(8,128)(2,1)}, bf16[768,512]{1,0:T(8,128)(2,1)S(1)}, u32[]{:S(2)}) copy-start(bf16[768,512]{1,0:T(8,128)(2,1)S(1)} %collective-permute-done.9.refs_17_.refs_21_.refs_26_.refs_30_) | copy-start | bytes 2359300
  73.0 34.2 %copy-start.13 = (bf16[512,1024]{1,0:T(8,128)(2,1)}, bf16[512,1024]{1,0:T(8,128)(2,1)S(1)}, u32[]{:S(2)}) copy-start(bf16[512,1024]{1,0:T(8,128)(2,1)S(1)} %collective-permute-done.12.refs_5_.refs_6_) | copy-start | bytes 3145732
  73.0 34.2 %copy-start.14 = (bf16[512,1024]{1,0:T(8,128)(2,1)}, bf16[512,1024]{1,0:T(8,128)(2,1)S(1)}, u32[]{:S(2)}) copy-start(bf16[512,1024]{1,0:T(8,128)(2,1)S(1)} %collective-permute-done.10.refs_2_.refs_3_) | copy-start | bytes 3145732
  79.6 20.8 %collective-permute-start.13 = (bf16[512,1024]{1,0:T(8,128)(2,1)S(1)}, bf16[512,1024]{1,0:T(8,128)(2,1)S(1)}, u32[]{:S(2)}, u32[]{:S(2)}) collective-permute-start(bf16[512,1024]{1,0:T(8,128)(2,1)S(1)} %collective-permute-done.10.refs_2_.refs_3_), channel_id=1, source_target_pairs={{0,16},{1,17},{2,18},{3,19},{4,20},{5,21},{6,22},{7,23},{8,24},{9,... | collective-permute-start | bytes 3145736 | tf_op jit(solution)/shard_map/ppermute | solution.py:93
  79.6 20.8 %collective-permute-start.14 = (bf16[512,1024]{1,0:T(8,128)(2,1)S(1)}, bf16[512,1024]{1,0:T(8,128)(2,1)S(1)}, u32[]{:S(2)}, u32[]{:S(2)}) collective-permute-start(bf16[512,1024]{1,0:T(8,128)(2,1)S(1)} %collective-permute-done.3.refs_3_.refs_4_), channel_id=1, source_target_pairs={{0,16},{1,17},{2,18},{3,19},{4,20},{5,21},{6,22},{7,23},{8,24},{9,... | collective-permute-start | bytes 3145736 | tf_op jit(solution)/shard_map/ppermute | solution.py:93
  80.2 20.3 %collective-permute-start.17 = (bf16[512,1024]{1,0:T(8,128)(2,1)}, bf16[512,1024]{1,0:T(8,128)(2,1)S(1)}, u32[]{:S(2)}, u32[]{:S(2)}) collective-permute-start(bf16[512,1024]{1,0:T(8,128)(2,1)} %collective-permute-done.8.refs_9_), channel_id=1, source_target_pairs={{0,16},{1,17},{2,18},{3,19},{4,20},{5,21},{6,22},{7,23},{8,24},{9,... | collective-permute-start | bytes 3145736 | tf_op jit(solution)/shard_map/ppermute | solution.py:93
  80.2 20.3 %collective-permute-start.15 = (bf16[768,512]{1,0:T(8,128)(2,1)}, bf16[768,512]{1,0:T(8,128)(2,1)}, u32[]{:S(2)}, u32[]{:S(2)}) collective-permute-start(bf16[768,512]{1,0:T(8,128)(2,1)} %refs_21_), channel_id=1, source_target_pairs={{0,3},{1,0},{2,1},{3,2},{4,7},{5,4},{6,5},{7,6},{8,11},{9,8},{10,9... | collective-permute-start | bytes 2359304 | tf_op jit(solution)/shard_map/ppermute | solution.py:99
  80.5 20.0 %collective-permute-start.16 = (bf16[768,512]{1,0:T(8,128)(2,1)S(1)}, bf16[768,512]{1,0:T(8,128)(2,1)S(1)}, u32[]{:S(2)}, u32[]{:S(2)}) collective-permute-start(bf16[768,512]{1,0:T(8,128)(2,1)S(1)} %collective-permute-done.9.refs_17_.refs_21_.refs_26_.refs_30_), channel_id=1, source_target_pairs={{0,4},{1,5},{2,6},{3,7},{4,8},{5,9},{6,10},{7,11},{8,12},{9,13},{1... | collective-permute-start | bytes 2359304 | tf_op jit(solution)/shard_map/ppermute | solution.py:93
  100.4 6.8 %copy-start.9 = (bf16[768,512]{1,0:T(8,128)(2,1)}, bf16[768,512]{1,0:T(8,128)(2,1)S(1)}, u32[]{:S(2)}) copy-start(bf16[768,512]{1,0:T(8,128)(2,1)S(1)} %collective-permute-done.16.refs_18_.refs_22_.refs_27_.refs_31_) | copy-start | bytes 2359300
  100.4 6.8 %copy-start.15 = (bf16[512,1024]{1,0:T(8,128)(2,1)}, bf16[512,1024]{1,0:T(8,128)(2,1)S(1)}, u32[]{:S(2)}) copy-start(bf16[512,1024]{1,0:T(8,128)(2,1)S(1)} %collective-permute-done.13.refs_6_.refs_7_) | copy-start | bytes 3145732
  100.5 6.8 %copy-start.16 = (bf16[512,1024]{1,0:T(8,128)(2,1)}, bf16[512,1024]{1,0:T(8,128)(2,1)S(1)}, u32[]{:S(2)}) copy-start(bf16[512,1024]{1,0:T(8,128)(2,1)S(1)} %collective-permute-done.14.refs_7_.refs_8_) | copy-start | bytes 3145732
  100.5 6.8 %copy-start.17 = (bf16[512,1024]{1,0:T(8,128)(2,1)}, bf16[512,1024]{1,0:T(8,128)(2,1)S(1)}, u32[]{:S(2)}) copy-start(bf16[512,1024]{1,0:T(8,128)(2,1)S(1)} %collective-permute-done.17.refs_13_) | copy-start | bytes 3145732
  100.5 27.5 %collective-permute-start.20 = (bf16[512,1024]{1,0:T(8,128)(2,1)}, bf16[512,1024]{1,0:T(8,128)(2,1)}, u32[]{:S(2)}, u32[]{:S(2)}) collective-permute-start(bf16[512,1024]{1,0:T(8,128)(2,1)} %collective-permute-done.8.refs_9_), channel_id=1, source_target_pairs={{0,32},{1,33},{2,34},{3,35},{4,36},{5,37},{6,38},{7,39},{8,40},{9,... | collective-permute-start | bytes 3145736 | tf_op jit(solution)/shard_map/ppermute | solution.py:93
  102.1 25.8 %collective-permute-start.21 = (bf16[512,1024]{1,0:T(8,128)(2,1)}, bf16[512,1024]{1,0:T(8,128)(2,1)}, u32[]{:S(2)}, u32[]{:S(2)}) collective-permute-start(bf16[512,1024]{1,0:T(8,128)(2,1)} %collective-permute-done.8.refs_9_), channel_id=1, source_target_pairs={{0,96},{1,97},{2,98},{3,99},{4,100},{5,101},{6,102},{7,103},{8,104... | collective-permute-start | bytes 3145736 | tf_op jit(solution)/shard_map/ppermute | solution.py:93
  103.8 19.5 %collective-permute-start.19 = (bf16[768,512]{1,0:T(8,128)(2,1)}, bf16[768,512]{1,0:T(8,128)(2,1)}, u32[]{:S(2)}, u32[]{:S(2)}) collective-permute-start(bf16[768,512]{1,0:T(8,128)(2,1)} %collective-permute-done.15.refs_33_), channel_id=1, source_target_pairs={{0,12},{1,13},{2,14},{3,15},{4,0},{5,1},{6,2},{7,3},{8,4},{9,5},{1... | collective-permute-start | bytes 2359304 | tf_op jit(solution)/shard_map/ppermute | solution.py:93
  106.3 17.0 %collective-permute-start.22 = (bf16[768,512]{1,0:T(8,128)(2,1)}, bf16[768,512]{1,0:T(8,128)(2,1)}, u32[]{:S(2)}, u32[]{:S(2)}) collective-permute-start(bf16[768,512]{1,0:T(8,128)(2,1)} %collective-permute-done.15.refs_33_), channel_id=1, source_target_pairs={{0,4},{1,5},{2,6},{3,7},{4,8},{5,9},{6,10},{7,11},{8,12},{9,13},{1... | collective-permute-start | bytes 2359304 | tf_op jit(solution)/shard_map/ppermute | solution.py:93
  106.3 19.9 %collective-permute-start.18 = (bf16[768,512]{1,0:T(8,128)(2,1)S(1)}, bf16[768,512]{1,0:T(8,128)(2,1)}, u32[]{:S(2)}, u32[]{:S(2)}) collective-permute-start(bf16[768,512]{1,0:T(8,128)(2,1)S(1)} %collective-permute-done.refs_16_.refs_20_.refs_25_.refs_29_), channel_id=1, source_target_pairs={{0,1},{1,2},{2,3},{3,0},{4,5},{5,6},{6,7},{7,4},{8,9},{9,10},{10,1... | collective-permute-start | bytes 2359304 | tf_op jit(solution)/shard_map/ppermute | solution.py:99
  110.0 44.5 %copy-start.22 = (s32[192]{0:T(256)S(1)}, s32[192]{0:T(256)}, u32[]{:S(2)}) copy-start(s32[192]{0:T(256)} %param.9) | copy-start | bytes 2308
  128.0 21.7 %collective-permute-start.24 = (bf16[512,1024]{1,0:T(8,128)(2,1)}, bf16[512,1024]{1,0:T(8,128)(2,1)}, u32[]{:S(2)}, u32[]{:S(2)}) collective-permute-start(bf16[512,1024]{1,0:T(8,128)(2,1)} %collective-permute-done.20.refs_10_), channel_id=1, source_target_pairs={{0,32},{1,33},{2,34},{3,35},{4,36},{5,37},{6,38},{7,39},{8,40},{9,... | collective-permute-start | bytes 3145736 | tf_op jit(solution)/shard_map/ppermute | solution.py:93
  128.0 21.7 %collective-permute-start.26 = (bf16[512,1024]{1,0:T(8,128)(2,1)}, bf16[512,1024]{1,0:T(8,128)(2,1)S(1)}, u32[]{:S(2)}, u32[]{:S(2)}) collective-permute-start(bf16[512,1024]{1,0:T(8,128)(2,1)} %collective-permute-done.20.refs_10_), channel_id=1, source_target_pairs={{0,16},{1,17},{2,18},{3,19},{4,20},{5,21},{6,22},{7,23},{8,24},{9,... | collective-permute-start | bytes 3145736 | tf_op jit(solution)/shard_map/ppermute | solution.py:93
  128.2 21.4 %collective-permute-start.27 = (bf16[512,1024]{1,0:T(8,128)(2,1)}, bf16[512,1024]{1,0:T(8,128)(2,1)S(1)}, u32[]{:S(2)}, u32[]{:S(2)}) collective-permute-start(bf16[512,1024]{1,0:T(8,128)(2,1)} %collective-permute-done.21.refs_12_), channel_id=1, source_target_pairs={{0,16},{1,17},{2,18},{3,19},{4,20},{5,21},{6,22},{7,23},{8,24},{9,... | collective-permute-start | bytes 3145736 | tf_op jit(solution)/shard_map/ppermute | solution.py:93
  128.5 20.6 %collective-permute-start.23 = (bf16[768,512]{1,0:T(8,128)(2,1)}, bf16[768,512]{1,0:T(8,128)(2,1)S(1)}, u32[]{:S(2)}, u32[]{:S(2)}) collective-permute-start(bf16[768,512]{1,0:T(8,128)(2,1)} %collective-permute-done.18.refs_37_), channel_id=1, source_target_pairs={{0,4},{1,5},{2,6},{3,7},{4,8},{5,9},{6,10},{7,11},{8,12},{9,13},{1... | collective-permute-start | bytes 2359304 | tf_op jit(solution)/shard_map/ppermute | solution.py:93
  129.4 20.2 %collective-permute-start.25 = (bf16[768,512]{1,0:T(8,128)(2,1)}, bf16[768,512]{1,0:T(8,128)(2,1)S(1)}, u32[]{:S(2)}, u32[]{:S(2)}) collective-permute-start(bf16[768,512]{1,0:T(8,128)(2,1)} %collective-permute-done.19.refs_35_), channel_id=1, source_target_pairs={{0,12},{1,13},{2,14},{3,15},{4,0},{5,1},{6,2},{7,3},{8,4},{9,5},{1... | collective-permute-start | bytes 2359304 | tf_op jit(solution)/shard_map/ppermute | solution.py:93
  149.1 5.6 %copy-start.20 = (bf16[768,512]{1,0:T(8,128)(2,1)}, bf16[768,512]{1,0:T(8,128)(2,1)S(1)}, u32[]{:S(2)}) copy-start(bf16[768,512]{1,0:T(8,128)(2,1)S(1)} %collective-permute-done.23.refs_38_) | copy-start | bytes 2359300
  149.6 4.8 %copy-start.21 = (bf16[768,512]{1,0:T(8,128)(2,1)}, bf16[768,512]{1,0:T(8,128)(2,1)S(1)}, u32[]{:S(2)}) copy-start(bf16[768,512]{1,0:T(8,128)(2,1)S(1)} %collective-permute-done.25.refs_36_) | copy-start | bytes 2359300
  149.7 4.8 %copy-start.19 = (bf16[512,1024]{1,0:T(8,128)(2,1)}, bf16[512,1024]{1,0:T(8,128)(2,1)S(1)}, u32[]{:S(2)}) copy-start(bf16[512,1024]{1,0:T(8,128)(2,1)S(1)} %collective-permute-done.27.refs_16_) | copy-start | bytes 3145732
  149.7 5.0 %collective-permute-start.28 = (bf16[512,1024]{1,0:T(8,128)(2,1)}, bf16[512,1024]{1,0:T(8,128)(2,1)}, u32[]{:S(2)}, u32[]{:S(2)}) collective-permute-start(bf16[512,1024]{1,0:T(8,128)(2,1)} %collective-permute-done.24.refs_11_), channel_id=1, source_target_pairs={{0,16},{1,17},{2,18},{3,19},{4,20},{5,21},{6,22},{7,23},{8,24},{9,... | collective-permute-start | bytes 3145736 | tf_op jit(solution)/shard_map/ppermute | solution.py:93
  150.6 21.1 %collective-permute-start.29 = (bf16[768,512]{1,0:T(8,128)(2,1)}, bf16[768,512]{1,0:T(8,128)(2,1)S(1)}, u32[]{:S(2)}, u32[]{:S(2)}) collective-permute-start(bf16[768,512]{1,0:T(8,128)(2,1)} %collective-permute-done.18.refs_37_), channel_id=1, source_target_pairs={{0,12},{1,13},{2,14},{3,15},{4,0},{5,1},{6,2},{7,3},{8,4},{9,5},{1... | collective-permute-start | bytes 2359304 | tf_op jit(solution)/shard_map/ppermute | solution.py:93
  154.4 17.6 %collective-permute-start.30 = (bf16[768,512]{1,0:T(8,128)(2,1)S(1)}, bf16[768,512]{1,0:T(8,128)(2,1)S(1)}, u32[]{:S(2)}, u32[]{:S(2)}) collective-permute-start(bf16[768,512]{1,0:T(8,128)(2,1)S(1)} %collective-permute-done.23.refs_38_), channel_id=1, source_target_pairs={{0,4},{1,5},{2,6},{3,7},{4,8},{5,9},{6,10},{7,11},{8,12},{9,13},{1... | collective-permute-start | bytes 2359304 | tf_op jit(solution)/shard_map/ppermute | solution.py:93
  154.7 17.4 %copy-start = (bf16[768,1024]{1,0:T(8,128)(2,1)S(1)}, bf16[768,1024]{1,0:T(8,128)(2,1)}, u32[]{:S(2)}) copy-start(bf16[768,1024]{1,0:T(8,128)(2,1)} %student_ref.1) | copy-start | bytes 4718596
  154.7 17.4 %copy-start.1 = (f32[8192]{0:T(1024)S(1)}, f32[8192]{0:T(1024)}, u32[]{:S(2)}) copy-start(f32[8192]{0:T(1024)} %param.6) | copy-start | bytes 98308
  154.7 17.4 %copy-start.2 = (s32[48]{0:T(128)S(1)}, s32[48]{0:T(128)}, u32[]{:S(2)}) copy-start(s32[48]{0:T(128)} %stack.151.plan_ref) | copy-start | bytes 580
  179.7 5.1 %collective-permute-start.31 = (f32[8,768]{1,0:T(8,128)S(1)}, f32[8,768]{1,0:T(8,128)S(1)}, u32[]{:S(2)}, u32[]{:S(2)}) collective-permute-start(f32[8,768]{1,0:T(8,128)S(1)} %get-tuple-element.56.own_ref), channel_id=1, source_target_pairs={{0,1},{1,0},{2,3},{3,2},{4,5},{5,4},{6,7},{7,6},{8,9},{9,8},{10,11... | collective-permute-start | bytes 73736 | tf_op jit(solution)/shard_map/ppermute | solution.py:483
  180.2 4.7 %collective-permute-start.32 = (f32[8,768]{1,0:T(8,128)S(1)}, f32[8,768]{1,0:T(8,128)S(1)}, u32[]{:S(2)}, u32[]{:S(2)}) collective-permute-start(f32[8,768]{1,0:T(8,128)S(1)} %get-tuple-element.56.own_ref), channel_id=1, source_target_pairs={{0,2},{1,3},{2,0},{3,1},{4,6},{5,7},{6,4},{7,5},{8,10},{9,11},{10,... | collective-permute-start | bytes 73736 | tf_op jit(solution)/shard_map/ppermute | solution.py:483
  182.5 5.6 %collective-permute-start.33 = (f32[8,768]{1,0:T(8,128)S(1)}, f32[8,768]{1,0:T(8,128)S(1)}, u32[]{:S(2)}, u32[]{:S(2)}) collective-permute-start(f32[8,768]{1,0:T(8,128)S(1)} %get-tuple-element.56.own_ref), channel_id=1, source_target_pairs={{0,3},{1,2},{2,1},{3,0},{4,7},{5,6},{6,5},{7,4},{8,11},{9,10},{10,... | collective-permute-start | bytes 73736 | tf_op jit(solution)/shard_map/ppermute | solution.py:483
  188.9 1.1 collective-permute-start.34
  190.0 7.4 %collective-permute-start.35 = (f32[1,128]{1,0:T(1,128)S(1)}, f32[1,128]{1,0:T(1,128)S(1)}, u32[]{:S(2)}, u32[]{:S(2)}) collective-permute-start(f32[1,128]{1,0:T(1,128)S(1)} %add.602), channel_id=1, source_target_pairs={{0,128},{16,144},{32,160},{48,176},{64,192},{80,208},{96,224},{112... | collective-permute-start | bytes 1544 | tf_op jit(solution)/shard_map/ppermute | solution.py:472
  197.4 4.8 %collective-permute-start.36 = (f32[1,128]{1,0:T(1,128)S(1)}, f32[1,128]{1,0:T(1,128)S(1)}, u32[]{:S(2)}, u32[]{:S(2)}) collective-permute-start(f32[1,128]{1,0:T(1,128)S(1)} %add.603), channel_id=1, source_target_pairs={{0,32},{16,48},{32,64},{48,80},{64,96},{80,112},{96,0},{112,16},{1... | collective-permute-start | bytes 1544 | tf_op jit(solution)/shard_map/ppermute | solution.py:472
  198.3 5.0 %collective-permute-start.37 = (f32[1,128]{1,0:T(1,128)S(1)}, f32[1,128]{1,0:T(1,128)S(1)}, u32[]{:S(2)}, u32[]{:S(2)}) collective-permute-start(f32[1,128]{1,0:T(1,128)S(1)} %add.603), channel_id=1, source_target_pairs={{0,64},{16,80},{32,96},{48,112},{64,0},{80,16},{96,32},{112,48},{1... | collective-permute-start | bytes 1544 | tf_op jit(solution)/shard_map/ppermute | solution.py:472
  201.5 3.5 %collective-permute-start.38 = (f32[1,128]{1,0:T(1,128)S(1)}, f32[1,128]{1,0:T(1,128)S(1)}, u32[]{:S(2)}, u32[]{:S(2)}) collective-permute-start(f32[1,128]{1,0:T(1,128)S(1)} %add.603), channel_id=1, source_target_pairs={{0,96},{16,112},{32,0},{48,16},{64,32},{80,48},{96,64},{112,80},{1... | collective-permute-start | bytes 1544 | tf_op jit(solution)/shard_map/ppermute | solution.py:472
  205.0 6.4 %collective-permute-start.39 = (f32[1,128]{1,0:T(1,128)S(1)}, f32[1,128]{1,0:T(1,128)S(1)}, u32[]{:S(2)}, u32[]{:S(2)}) collective-permute-start(f32[1,128]{1,0:T(1,128)S(1)} %add_add_fusion.1), channel_id=1, source_target_pairs={{0,4},{1,5},{2,6},{3,7},{4,8},{5,9},{6,10},{7,11},{8,12},{9,13},{1... | collective-permute-start | bytes 1544 | tf_op jit(solution)/shard_map/ppermute | solution.py:472
  206.3 5.2 %collective-permute-start.40 = (f32[1,128]{1,0:T(1,128)S(1)}, f32[1,128]{1,0:T(1,128)S(1)}, u32[]{:S(2)}, u32[]{:S(2)}) collective-permute-start(f32[1,128]{1,0:T(1,128)S(1)} %add_add_fusion.1), channel_id=1, source_target_pairs={{0,8},{1,9},{2,10},{3,11},{4,12},{5,13},{6,14},{7,15},{8,0},{9,1},... | collective-permute-start | bytes 1544 | tf_op jit(solution)/shard_map/ppermute | solution.py:472
  210.0 3.5 %collective-permute-start.41 = (f32[1,128]{1,0:T(1,128)S(1)}, f32[1,128]{1,0:T(1,128)S(1)}, u32[]{:S(2)}, u32[]{:S(2)}) collective-permute-start(f32[1,128]{1,0:T(1,128)S(1)} %add_add_fusion.1), channel_id=1, source_target_pairs={{0,12},{1,13},{2,14},{3,15},{4,0},{5,1},{6,2},{7,3},{8,4},{9,5},{1... | collective-permute-start | bytes 1544 | tf_op jit(solution)/shard_map/ppermute | solution.py:472
  (1 other events, 1.0 us)

commit v2 on v0

--- a/solution.py
+++ b/solution.py
@@ -102,14 +102,14 @@
 
     here1, half_way, own, *_ = lax.optimization_barrier((z1, half_way, own, second0, third0))
     first1, second1 = first(here1), second(here1)
-    third1 = first(first1)
     far = far_hop(half_way)
 
-    far, here1, own, *_ = lax.optimization_barrier((far, here1, own, second1, third1))
+    far, here1, own, on1, *_ = lax.optimization_barrier((far, here1, own, first1, second1))
     far = widen(far)
     z3 = z_hop(own, -1)
-
-    here3, here1 = lax.optimization_barrier((z3, here1))
+    third1 = first(on1)
+
+    here3, here1, third1 = lax.optimization_barrier((z3, here1, third1))
     z2 = z_hop(here1, 1)
     first3, second3 = first(here3), second(here3)
     groups = [[own, first0, third0, second0], [here1, first1, third1, second1]]
@@ -157,7 +157,7 @@
     blocks = [[refs.pop(0) for _ in range(n)] for n in choices]
     out_ref = refs.pop(0)
     stats_ref = refs.pop(0) if last else None
-    total_ref, a_vm, w_vm, a_sem, w_sem, state_sem, *extra = refs
+    total_ref, a_vm, w_vm, a_sem, w_sem, state_sem, out_sem, *extra = refs
     tok, width = total_ref.shape
     cols = width - 128
 
@@ -231,18 +231,26 @@
             square += state_vm[rows, cols:]
             stats_ref[:, rows] = statistics(total, square, stud_vm[rows, :], out_ref, rows)
         return
+    start(1)
     if first:
-        state = pltpu.make_async_copy(state_ref.at[pl.ds(0, tok)], total_ref, state_sem)
+        (state_vm,) = extra
+        state = pltpu.make_async_copy(state_ref.at[pl.ds(0, tok)], state_vm, state_sem)
         state.start()
-        start(1)
+    total_ref[...] = jnp.zeros_like(total_ref)
+    lax.fori_loop(0, count, whole_step, 0)
+    if first:
         state.wait()
-    else:
-        start(1)
-        total_ref[...] = jnp.zeros_like(total_ref)
-    lax.fori_loop(0, count, whole_step, 0)
-    result = pltpu.make_async_copy(total_ref, out_ref.at[pl.ds(0, tok)], state_sem)
-    result.start()
-    result.wait()
+    copies = []
+    for r in range(0, tok, CHUNK):
+        rows = pl.ds(r, CHUNK)
+        if first:
+            total_ref[rows, :] += state_vm[rows, :]
+        copies.append(
+            pltpu.make_async_copy(total_ref.at[rows], out_ref.at[rows], out_sem.at[r // CHUNK])
+        )
+        copies[-1].start()
+    for copy in copies:
+        copy.wait()
 
 
 def statistics(logits, square, student, out_ref, rows):
@@ -283,10 +291,12 @@
         pltpu.SemaphoreType.DMA((count,)),
         pltpu.SemaphoreType.DMA((count,)),
         pltpu.SemaphoreType.DMA,
+        pltpu.SemaphoreType.DMA((tok // CHUNK,)),
     ]
+    if first:
+        scratch += [pltpu.VMEM((tok, cols + 128), jnp.float32)]
     if last:
         scratch += [
-            pltpu.VMEM((tok, cols + 128), jnp.float32),
             pltpu.VMEM((tok, cols), jnp.bfloat16),
             pltpu.SemaphoreType.DMA,
         ]

time: 213 us -> 214 us (level)
  waiting for transfers between devices: 102 us -> 106 us
    ppermute x2, waiting for transfers between devices: 7.77 us -> 3.29 us  [far_hop(): return lax.ppermute(value, ('rows', 'tp'), whole(z_two))]
    ppermute x5, waiting for transfers between devices: 22.3 us -> 26.2 us  [second(): return lax.ppermute(value, ('rows', 'tp'), whole(x_second))]
    ppermute x3, waiting for transfers between devices: 35.4 us -> 38.7 us  [z_hop(): return lax.ppermute(value, 'tp', z_ring(d))]
  transfers between devices with their start and end apart: 30 -> 30, of which waited for: 14 -> 16; matrix products, arithmetic and copies ran while one was open for 1% -> 1% of each run, Pallas kernels for 13% -> 12%
where the time goes in v2:
time: 214 us; the launch traced here: 213 us
  waiting for transfers between devices  106 us (50%)
  starting transfers between devices  53.5 us (25%)
  Pallas kernels  32.6 us (15%)
  between operations  16.5 us (8%)
  local copies, waits for them, and re-layouts  3.32 us (2%)
    ppermute x3, waiting for transfers between devices, z_hop(): return lax.ppermute(value, 'tp', z_ring(d))  38.7 us
    ppermute x7, waiting for transfers between devices, first(): return lax.ppermute(value, ('rows', 'tp'), whole(x_first))  29.7 us
    pallas_call x3, Pallas kernels, accumulate_blocks(): pl.pallas_call(functools.partial(teacher_kernel, first, [len(block) for b...  29.3 us
    ppermute x5, waiting for transfers between devices, second(): return lax.ppermute(value, ('rows', 'tp'), whole(x_second))  26.2 us
    ppermute x8, starting transfers between devices, stage(): return sum([lax.ppermute(value, axis, move) for move in moves], value)  19 us
    ppermute x7, starting transfers between devices, first(): return lax.ppermute(value, ('rows', 'tp'), whole(x_first))  9.86 us
    ppermute x3, starting transfers between devices, z_hop(): return lax.ppermute(value, 'tp', z_ring(d))  7.11 us
    ppermute x2, starting transfers between devices, far_hop(): return lax.ppermute(value, ('rows', 'tp'), whole(z_two))  6.62 us
  transfers between devices with their start and end apart: 30, of which 16 were waited for; matrix products, arithmetic and copies ran while one was open for 1% of the time, Pallas kernels for 12%

profile of v2, /device:TPU:2, one launch (start us, length us, event | category | flops | bytes accessed | tf_op | source)
XLA Modules:
  0.0 212.7 jit_solution(5523416154193913902)
XLA Ops:
  7.2 0.0 all-gather.5.cloned.1.call-start
  7.2 0.7 all-gather.5.cloned.1.call-update
  7.9 0.0 all-gather.7.cloned.1.call-start
  7.9 1.6 collective-permute-start.3
  9.5 3.3 %collective-permute-start.1 = (bf16[512,1024]{1,0:T(8,128)(2,1)}, bf16[512,1024]{1,0:T(8,128)(2,1)S(1)}, u32[]{:S(2)}, u32[]{:S(2)}) collective-permute-start(bf16[512,1024]{1,0:T(8,128)(2,1)} %param.7), channel_id=1, source_target_pairs={{0,2},{1,3},{2,128},{3,129},{4,6},{5,7},{6,132},{7,133},{8,10},{9,... | collective-permute-start | bytes 3145736 | tf_op jit(solution)/shard_map/ppermute | solution.py:89
  12.8 0.5 collective-permute-start.2
  13.3 1.9 collective-permute-start
  15.2 7.7 %collective-permute-done.3.refs_1_.refs_5_.refs_2_.refs_6_ = bf16[768,512]{1,0:T(8,128)(2,1)S(1)} collective-permute-done((bf16[768,512]{1,0:T(8,128)(2,1)}, bf16[768,512]{1,0:T(8,128)(2,1)S(1)}, u32[]{:S(2)}, u32[]{:S(2)}) %collective-permute-start.3) | collective-permute-done | bytes 786464 | tf_op jit(solution)/shard_map/ppermute | solution.py:83
  22.9 2.0 collective-permute-start.4
  24.9 5.8 %collective-permute-done.2.refs_3_.refs_7_.refs_4_.refs_8_ = bf16[768,512]{1,0:T(8,128)(2,1)S(1)} collective-permute-done((bf16[768,512]{1,0:T(8,128)(2,1)}, bf16[768,512]{1,0:T(8,128)(2,1)S(1)}, u32[]{:S(2)}, u32[]{:S(2)}) %collective-permute-start.2) | collective-permute-done | bytes 786464 | tf_op jit(solution)/shard_map/ppermute | solution.py:86
  30.7 22.8 %collective-permute-done.refs_8_.refs_12_.refs_9_.refs_13_ = bf16[768,512]{1,0:T(8,128)(2,1)S(1)} collective-permute-done((bf16[768,512]{1,0:T(8,128)(2,1)}, bf16[768,512]{1,0:T(8,128)(2,1)S(1)}, u32[]{:S(2)}, u32[]{:S(2)}) %collective-permute-start) | collective-permute-done | bytes 786464 | tf_op jit(solution)/shard_map/ppermute | solution.py:92
  53.5 0.0 collective-permute-done.1
  53.5 3.3 %collective-permute-start.5 = (bf16[512,1024]{1,0:T(8,128)(2,1)S(1)}, bf16[512,1024]{1,0:T(8,128)(2,1)}, u32[]{:S(2)}, u32[]{:S(2)}) collective-permute-start(bf16[512,1024]{1,0:T(8,128)(2,1)S(1)} %collective-permute-done.1), channel_id=1, source_target_pairs={{0,2},{1,3},{2,128},{3,129},{4,6},{5,7},{6,132},{7,133},{8,10},{9,... | collective-permute-start | bytes 3145736 | tf_op jit(solution)/shard_map/ppermute | solution.py:89
  56.9 1.2 collective-permute-start.6
  58.1 0.8 collective-permute-start.7
  58.9 16.5 %collective-permute-done.6.refs_9_.refs_13_.refs_10_.refs_14_ = bf16[768,512]{1,0:T(8,128)(2,1)} collective-permute-done((bf16[768,512]{1,0:T(8,128)(2,1)S(1)}, bf16[768,512]{1,0:T(8,128)(2,1)}, u32[]{:S(2)}, u32[]{:S(2)}) %collective-permute-start.6) | collective-permute-done | bytes 786464 | tf_op jit(solution)/shard_map/ppermute | solution.py:83
  75.5 0.9 copy-done.7
  76.3 3.3 %collective-permute-done.5 = bf16[512,1024]{1,0:T(8,128)(2,1)} collective-permute-done((bf16[512,1024]{1,0:T(8,128)(2,1)S(1)}, bf16[512,1024]{1,0:T(8,128)(2,1)}, u32[]{:S(2)}, u32[]{:S(2)}) %collective-permute-start.5) | collective-permute-done | bytes 1048608 | tf_op jit(solution)/shard_map/ppermute | solution.py:89
  79.6 0.0 all-gather.7.cloned.1.call-update
  79.7 4.0 %collective-permute-start.8 = (bf16[768,512]{1,0:T(8,128)(2,1)}, bf16[768,512]{1,0:T(8,128)(2,1)}, u32[]{:S(2)}, u32[]{:S(2)}) collective-permute-start(bf16[768,512]{1,0:T(8,128)(2,1)} %refs_5_), channel_id=1, source_target_pairs={{0,3},{1,0},{2,1},{3,2},{4,7},{5,4},{6,5},{7,6},{8,11},{9,8},{10,9... | collective-permute-start | bytes 2359304 | tf_op jit(solution)/shard_map/ppermute | solution.py:92
  83.6 1.5 collective-permute-start.9
  85.2 14.3 %collective-permute-done.8.refs_17_ = bf16[768,512]{1,0:T(8,128)(2,1)} collective-permute-done((bf16[768,512]{1,0:T(8,128)(2,1)}, bf16[768,512]{1,0:T(8,128)(2,1)}, u32[]{:S(2)}, u32[]{:S(2)}) %collective-permute-start.8) | collective-permute-done | bytes 786464 | tf_op jit(solution)/shard_map/ppermute | solution.py:92
  99.4 1.5 collective-permute-start.10
  100.9 2.2 %collective-permute-start.11 = (bf16[768,512]{1,0:T(8,128)(2,1)}, bf16[768,512]{1,0:T(8,128)(2,1)}, u32[]{:S(2)}, u32[]{:S(2)}) collective-permute-start(bf16[768,512]{1,0:T(8,128)(2,1)} %collective-permute-done.8.refs_17_), channel_id=1, source_target_pairs={{0,12},{1,13},{2,14},{3,15},{4,0},{5,1},{6,2},{7,3},{8,4},{9,5},{1... | collective-permute-start | bytes 2359304 | tf_op jit(solution)/shard_map/ppermute | solution.py:86
  103.1 1.2 collective-permute-start.12
  104.3 0.7 stack.151.plan_ref
  105.1 0.0 copy-start.11
  105.1 8.3 %teacher_0.1.refs_0_ = f32[6144,1152]{1,0:T(8,128)} custom-call(s32[48]{0:T(128)} %stack.151.plan_ref, f32[16,1,512]{2,1,0:T(1,128)} %bitcast.41, bf16[8,512,1024]{2,1,0:T(8,128)(2,1)} %bitcast.44, bf16[8,512,1024]{2,1,0:T(8,128)(2,1)} %bitcast.45, bf16[768,512]{1,0:T(8,128)(2,1)} %refs_5_, bf16[768,512]{1,0:T(8,128)(2,1)} %copy-done.3, ...), custom_call_target="tpu_custom_call" | custom-call | tf_op jit(solution)/shard_map/teacher_0/pallas_call | solution.py:304
  113.3 5.5 %collective-permute-done.10.refs_18_ = bf16[768,512]{1,0:T(8,128)(2,1)} collective-permute-done((bf16[768,512]{1,0:T(8,128)(2,1)}, bf16[768,512]{1,0:T(8,128)(2,1)}, u32[]{:S(2)}, u32[]{:S(2)}) %collective-permute-start.10) | collective-permute-done | bytes 786464 | tf_op jit(solution)/shard_map/ppermute | solution.py:83
  118.9 1.6 collective-permute-done.12.refs_21_
  120.4 1.7 collective-permute-start.13
  122.2 0.3 collective-permute-start.14
  122.5 18.0 %collective-permute-done.13.refs_20_ = bf16[768,512]{1,0:T(8,128)(2,1)S(1)} collective-permute-done((bf16[768,512]{1,0:T(8,128)(2,1)}, bf16[768,512]{1,0:T(8,128)(2,1)S(1)}, u32[]{:S(2)}, u32[]{:S(2)}) %collective-permute-start.13) | collective-permute-done | bytes 786464 | tf_op jit(solution)/shard_map/ppermute | solution.py:86
  140.4 0.9 copy-done.10
  141.3 0.3 collective-permute-start.15
  141.6 1.8 collective-permute-start.16
  143.4 0.1 broadcast_in_dim.3
  143.5 0.1 reshape.55
  143.6 0.0 all-gather.7.cloned.1.call-done
  143.6 0.0 copy-start
  143.6 0.0 copy-start.1
  143.7 15.0 %teacher_4.1.refs_1_ = f32[6144,1152]{1,0:T(8,128)} custom-call(s32[48]{0:T(128)} %stack.151.plan_ref, f32[16,1,512]{2,1,0:T(1,128)} %bitcast.42, bf16[8,512,1024]{2,1,0:T(8,128)(2,1)} %bitcast.46, bf16[8,512,1024]{2,1,0:T(8,128)(2,1)} %bitcast.48, f32[6144,1152]{1,0:T(8,128)} %teacher_0.1.refs_0_, bf16[768,512]{1,0:T(8,128)(2,1)} %refs_5_, ...), custom_call_target="tpu_custom_call" | custom-call | tf_op jit(solution)/shard_map/teacher_4/pallas_call | solution.py:304
  158.7 2.5 %collective-permute-done.15.refs_2_ = bf16[768,512]{1,0:T(8,128)(2,1)S(1)} collective-permute-done((bf16[768,512]{1,0:T(8,128)(2,1)}, bf16[768,512]{1,0:T(8,128)(2,1)S(1)}, u32[]{:S(2)}, u32[]{:S(2)}) %collective-permute-start.15) | collective-permute-done | bytes 786464 | tf_op jit(solution)/shard_map/ppermute | solution.py:86
  161.2 6.0 %teacher_14.1 = (f32[768,1024]{1,0:T(8,128)S(1)}, f32[8,768]{1,0:T(8,128)S(1)}) custom-call(s32[48]{0:T(128)S(1)} %copy-done.2, f32[16,1,512]{2,1,0:T(1,128)S(1)} %bitcast.43, bf16[8,512,1024]{2,1,0:T(8,128)(2,1)} %bitcast.47, bf16[8,512,1024]{2,1,0:T(8,128)(2,1)} %bitcast.49, bf16[768,1024]{1,0:T(8,128)(2,1)S(1)} %copy-done, ...), custom_call_target="tpu_custom_call" | custom-call | tf_op jit(solution)/shard_map/teacher_14/pallas_call | solution.py:304
  167.2 2.9 %collective-permute-start.17 = (f32[8,768]{1,0:T(8,128)S(1)}, f32[8,768]{1,0:T(8,128)S(1)}, u32[]{:S(2)}, u32[]{:S(2)}) collective-permute-start(f32[8,768]{1,0:T(8,128)S(1)} %get-tuple-element.36.own_ref), channel_id=1, source_target_pairs={{0,1},{1,0},{2,3},{3,2},{4,5},{5,4},{6,7},{7,6},{8,9},{9,8},{10,11... | collective-permute-start | bytes 73736 | tf_op jit(solution)/shard_map/ppermute | solution.py:401
  170.1 2.5 %collective-permute-start.19 = (f32[8,768]{1,0:T(8,128)S(1)}, f32[8,768]{1,0:T(8,128)S(1)}, u32[]{:S(2)}, u32[]{:S(2)}) collective-permute-start(f32[8,768]{1,0:T(8,128)S(1)} %get-tuple-element.36.own_ref), channel_id=1, source_target_pairs={{0,3},{1,2},{2,1},{3,0},{4,7},{5,6},{6,5},{7,4},{8,11},{9,10},{10,... | collective-permute-start | bytes 73736 | tf_op jit(solution)/shard_map/ppermute | solution.py:401
  172.5 0.6 convert_reduce_fusion
  173.1 1.9 collective-permute-done.18.third_ref
  175.0 0.7 collective-permute-done.19.fourth_ref
  175.7 0.8 combine.1
  176.5 0.2 collective-permute-start.20
  176.7 1.1 collective-permute-done.20
  177.8 8.0 %collective-permute-start.21 = (f32[1,128]{1,0:T(1,128)S(1)}, f32[1,128]{1,0:T(1,128)S(1)}, u32[]{:S(2)}, u32[]{:S(2)}) collective-permute-start(f32[1,128]{1,0:T(1,128)S(1)} %add.374), channel_id=1, source_target_pairs={{0,128},{16,144},{32,160},{48,176},{64,192},{80,208},{96,224},{112... | collective-permute-start | bytes 1544 | tf_op jit(solution)/shard_map/ppermute | solution.py:390
  185.8 2.6 %gradient.1 = bf16[768,1024]{1,0:T(8,128)(2,1)} custom-call(f32[8,768]{1,0:T(8,128)S(1)} %get-tuple-element.38.coef_ref, f32[768,1024]{1,0:T(8,128)S(1)} %get-tuple-element.39.teach_ref, bf16[768,1024]{1,0:T(8,128)(2,1)S(1)} %copy-done), custom_call_target="tpu_custom_call" | custom-call | tf_op jit(solution)/shard_map/gradient/pallas_call | solution.py:378
  188.3 1.4 collective-permute-start.22
  189.7 3.1 %collective-permute-start.23 = (f32[1,128]{1,0:T(1,128)S(1)}, f32[1,128]{1,0:T(1,128)S(1)}, u32[]{:S(2)}, u32[]{:S(2)}) collective-permute-start(f32[1,128]{1,0:T(1,128)S(1)} %add.375), channel_id=1, source_target_pairs={{0,64},{16,80},{32,96},{48,112},{64,0},{80,16},{96,32},{112,48},{1... | collective-permute-start | bytes 1544 | tf_op jit(solution)/shard_map/ppermute | solution.py:390
  192.8 1.1 collective-permute-start.24
  194.0 0.8 collective-permute-done.23
  194.7 1.6 collective-permute-done.24
  196.4 1.5 collective-permute-start.25
  197.9 1.4 collective-permute-start.26
  199.3 2.2 %collective-permute-start.27 = (f32[1,128]{1,0:T(1,128)S(1)}, f32[1,128]{1,0:T(1,128)S(1)}, u32[]{:S(2)}, u32[]{:S(2)}) collective-permute-start(f32[1,128]{1,0:T(1,128)S(1)} %add_add_fusion.1), channel_id=1, source_target_pairs={{0,12},{1,13},{2,14},{3,15},{4,0},{5,1},{6,2},{7,3},{8,4},{9,5},{1... | collective-permute-start | bytes 1544 | tf_op jit(solution)/shard_map/ppermute | solution.py:390
  201.5 1.4 collective-permute-done.26
  203.0 0.6 fusion
  (37 shorter events, 0.1 us)
Async XLA Ops:
  7.2 97.9 %all-gather.5.cloned.1.call-start = ((), (), s32[]{:S(2)}) async-start(), calls=%async_computation | async-start | bytes 9437184 | tf_op jit(solution)/shard_map/all_gather | solution.py:95
  7.9 135.7 %all-gather.7.cloned.1.call-start = ((), (), s32[]{:S(2)}) async-start(), calls=%async_computation.1 | async-start | bytes 9437184 | tf_op jit(solution)/shard_map/all_gather | solution.py:95
  7.9 15.0 %collective-permute-start.3 = (bf16[768,512]{1,0:T(8,128)(2,1)}, bf16[768,512]{1,0:T(8,128)(2,1)S(1)}, u32[]{:S(2)}, u32[]{:S(2)}) collective-permute-start(bf16[768,512]{1,0:T(8,128)(2,1)} %refs_5_), channel_id=1, source_target_pairs={{0,4},{1,5},{2,6},{3,7},{4,8},{5,9},{6,10},{7,11},{8,12},{9,13},{1... | collective-permute-start | bytes 2359304 | tf_op jit(solution)/shard_map/ppermute | solution.py:83
  9.5 44.0 %collective-permute-start.1 = (bf16[512,1024]{1,0:T(8,128)(2,1)}, bf16[512,1024]{1,0:T(8,128)(2,1)S(1)}, u32[]{:S(2)}, u32[]{:S(2)}) collective-permute-start(bf16[512,1024]{1,0:T(8,128)(2,1)} %param.7), channel_id=1, source_target_pairs={{0,2},{1,3},{2,128},{3,129},{4,6},{5,7},{6,132},{7,133},{8,10},{9,... | collective-permute-start | bytes 3145736 | tf_op jit(solution)/shard_map/ppermute | solution.py:89
  12.8 17.9 %collective-permute-start.2 = (bf16[768,512]{1,0:T(8,128)(2,1)}, bf16[768,512]{1,0:T(8,128)(2,1)S(1)}, u32[]{:S(2)}, u32[]{:S(2)}) collective-permute-start(bf16[768,512]{1,0:T(8,128)(2,1)} %refs_5_), channel_id=1, source_target_pairs={{0,12},{1,13},{2,14},{3,15},{4,0},{5,1},{6,2},{7,3},{8,4},{9,5},{1... | collective-permute-start | bytes 2359304 | tf_op jit(solution)/shard_map/ppermute | solution.py:86
  13.3 40.2 %collective-permute-start = (bf16[768,512]{1,0:T(8,128)(2,1)}, bf16[768,512]{1,0:T(8,128)(2,1)S(1)}, u32[]{:S(2)}, u32[]{:S(2)}) collective-permute-start(bf16[768,512]{1,0:T(8,128)(2,1)} %refs_5_), channel_id=1, source_target_pairs={{0,1},{1,2},{2,3},{3,0},{4,5},{5,6},{6,7},{7,4},{8,9},{9,10},{10,1... | collective-permute-start | bytes 2359304 | tf_op jit(solution)/shard_map/ppermute | solution.py:92
  22.9 82.1 %copy-start.3 = (bf16[768,512]{1,0:T(8,128)(2,1)}, bf16[768,512]{1,0:T(8,128)(2,1)S(1)}, u32[]{:S(2)}) copy-start(bf16[768,512]{1,0:T(8,128)(2,1)S(1)} %collective-permute-done.3.refs_1_.refs_5_.refs_2_.refs_6_) | copy-start | bytes 2359300
  22.9 30.6 %collective-permute-start.4 = (bf16[768,512]{1,0:T(8,128)(2,1)S(1)}, bf16[768,512]{1,0:T(8,128)(2,1)S(1)}, u32[]{:S(2)}, u32[]{:S(2)}) collective-permute-start(bf16[768,512]{1,0:T(8,128)(2,1)S(1)} %collective-permute-done.3.refs_1_.refs_5_.refs_2_.refs_6_), channel_id=1, source_target_pairs={{0,4},{1,5},{2,6},{3,7},{4,8},{5,9},{6,10},{7,11},{8,12},{9,13},{1... | collective-permute-start | bytes 2359304 | tf_op jit(solution)/shard_map/ppermute | solution.py:83
  30.7 74.4 %copy-start.4 = (bf16[768,512]{1,0:T(8,128)(2,1)}, bf16[768,512]{1,0:T(8,128)(2,1)S(1)}, u32[]{:S(2)}) copy-start(bf16[768,512]{1,0:T(8,128)(2,1)S(1)} %collective-permute-done.2.refs_3_.refs_7_.refs_4_.refs_8_) | copy-start | bytes 2359300
  53.5 51.5 %copy-start.5 = (bf16[768,512]{1,0:T(8,128)(2,1)}, bf16[768,512]{1,0:T(8,128)(2,1)S(1)}, u32[]{:S(2)}) copy-start(bf16[768,512]{1,0:T(8,128)(2,1)S(1)} %collective-permute-done.refs_8_.refs_12_.refs_9_.refs_13_) | copy-start | bytes 2359300
  53.5 51.5 %copy-start.6 = (bf16[768,512]{1,0:T(8,128)(2,1)}, bf16[768,512]{1,0:T(8,128)(2,1)S(1)}, u32[]{:S(2)}) copy-start(bf16[768,512]{1,0:T(8,128)(2,1)S(1)} %collective-permute-done.4.refs_2_.refs_6_.refs_3_.refs_7_) | copy-start | bytes 2359300
  53.5 26.1 %collective-permute-start.5 = (bf16[512,1024]{1,0:T(8,128)(2,1)S(1)}, bf16[512,1024]{1,0:T(8,128)(2,1)}, u32[]{:S(2)}, u32[]{:S(2)}) collective-permute-start(bf16[512,1024]{1,0:T(8,128)(2,1)S(1)} %collective-permute-done.1), channel_id=1, source_target_pairs={{0,2},{1,3},{2,128},{3,129},{4,6},{5,7},{6,132},{7,133},{8,10},{9,... | collective-permute-start | bytes 3145736 | tf_op jit(solution)/shard_map/ppermute | solution.py:89
  56.9 18.6 %collective-permute-start.6 = (bf16[768,512]{1,0:T(8,128)(2,1)S(1)}, bf16[768,512]{1,0:T(8,128)(2,1)}, u32[]{:S(2)}, u32[]{:S(2)}) collective-permute-start(bf16[768,512]{1,0:T(8,128)(2,1)S(1)} %collective-permute-done.refs_8_.refs_12_.refs_9_.refs_13_), channel_id=1, source_target_pairs={{0,4},{1,5},{2,6},{3,7},{4,8},{5,9},{6,10},{7,11},{8,12},{9,13},{1... | collective-permute-start | bytes 2359304 | tf_op jit(solution)/shard_map/ppermute | solution.py:83
  58.1 17.4 %collective-permute-start.7 = (bf16[768,512]{1,0:T(8,128)(2,1)S(1)}, bf16[768,512]{1,0:T(8,128)(2,1)S(1)}, u32[]{:S(2)}, u32[]{:S(2)}) collective-permute-start(bf16[768,512]{1,0:T(8,128)(2,1)S(1)} %collective-permute-done.refs_8_.refs_12_.refs_9_.refs_13_), channel_id=1, source_target_pairs={{0,12},{1,13},{2,14},{3,15},{4,0},{5,1},{6,2},{7,3},{8,4},{9,5},{1... | collective-permute-start | bytes 2359304 | tf_op jit(solution)/shard_map/ppermute | solution.py:86
  75.5 0.9 copy-start.7
  79.7 19.8 %collective-permute-start.8 = (bf16[768,512]{1,0:T(8,128)(2,1)}, bf16[768,512]{1,0:T(8,128)(2,1)}, u32[]{:S(2)}, u32[]{:S(2)}) collective-permute-start(bf16[768,512]{1,0:T(8,128)(2,1)} %refs_5_), channel_id=1, source_target_pairs={{0,3},{1,0},{2,1},{3,2},{4,7},{5,4},{6,5},{7,6},{8,11},{9,8},{10,9... | collective-permute-start | bytes 2359304 | tf_op jit(solution)/shard_map/ppermute | solution.py:92
  83.6 15.8 %collective-permute-start.9 = (bf16[768,512]{1,0:T(8,128)(2,1)}, bf16[768,512]{1,0:T(8,128)(2,1)S(1)}, u32[]{:S(2)}, u32[]{:S(2)}) collective-permute-start(bf16[768,512]{1,0:T(8,128)(2,1)} %collective-permute-done.6.refs_9_.refs_13_.refs_10_.refs_14_), channel_id=1, source_target_pairs={{0,4},{1,5},{2,6},{3,7},{4,8},{5,9},{6,10},{7,11},{8,12},{9,13},{1... | collective-permute-start | bytes 2359304 | tf_op jit(solution)/shard_map/ppermute | solution.py:83
  99.4 1.5 copy-start.8
  99.4 19.4 %collective-permute-start.10 = (bf16[768,512]{1,0:T(8,128)(2,1)}, bf16[768,512]{1,0:T(8,128)(2,1)}, u32[]{:S(2)}, u32[]{:S(2)}) collective-permute-start(bf16[768,512]{1,0:T(8,128)(2,1)} %collective-permute-done.8.refs_17_), channel_id=1, source_target_pairs={{0,4},{1,5},{2,6},{3,7},{4,8},{5,9},{6,10},{7,11},{8,12},{9,13},{1... | collective-permute-start | bytes 2359304 | tf_op jit(solution)/shard_map/ppermute | solution.py:83
  100.9 17.9 %collective-permute-start.11 = (bf16[768,512]{1,0:T(8,128)(2,1)}, bf16[768,512]{1,0:T(8,128)(2,1)}, u32[]{:S(2)}, u32[]{:S(2)}) collective-permute-start(bf16[768,512]{1,0:T(8,128)(2,1)} %collective-permute-done.8.refs_17_), channel_id=1, source_target_pairs={{0,12},{1,13},{2,14},{3,15},{4,0},{5,1},{6,2},{7,3},{8,4},{9,5},{1... | collective-permute-start | bytes 2359304 | tf_op jit(solution)/shard_map/ppermute | solution.py:86
  103.1 17.3 %collective-permute-start.12 = (bf16[768,512]{1,0:T(8,128)(2,1)S(1)}, bf16[768,512]{1,0:T(8,128)(2,1)}, u32[]{:S(2)}, u32[]{:S(2)}) collective-permute-start(bf16[768,512]{1,0:T(8,128)(2,1)S(1)} %collective-permute-done.refs_8_.refs_12_.refs_9_.refs_13_), channel_id=1, source_target_pairs={{0,1},{1,2},{2,3},{3,0},{4,5},{5,6},{6,7},{7,4},{8,9},{9,10},{10,1... | collective-permute-start | bytes 2359304 | tf_op jit(solution)/shard_map/ppermute | solution.py:92
  105.1 38.3 %copy-start.11 = (s32[192]{0:T(256)S(1)}, s32[192]{0:T(256)}, u32[]{:S(2)}) copy-start(s32[192]{0:T(256)} %param.9) | copy-start | bytes 2308
  120.4 20.0 %collective-permute-start.13 = (bf16[768,512]{1,0:T(8,128)(2,1)}, bf16[768,512]{1,0:T(8,128)(2,1)S(1)}, u32[]{:S(2)}, u32[]{:S(2)}) collective-permute-start(bf16[768,512]{1,0:T(8,128)(2,1)} %collective-permute-done.11.refs_19_), channel_id=1, source_target_pairs={{0,12},{1,13},{2,14},{3,15},{4,0},{5,1},{6,2},{7,3},{8,4},{9,5},{1... | collective-permute-start | bytes 2359304 | tf_op jit(solution)/shard_map/ppermute | solution.py:86
  122.2 18.3 %collective-permute-start.14 = (bf16[768,512]{1,0:T(8,128)(2,1)}, bf16[768,512]{1,0:T(8,128)(2,1)S(1)}, u32[]{:S(2)}, u32[]{:S(2)}) collective-permute-start(bf16[768,512]{1,0:T(8,128)(2,1)} %collective-permute-done.12.refs_21_), channel_id=1, source_target_pairs={{0,4},{1,5},{2,6},{3,7},{4,8},{5,9},{6,10},{7,11},{8,12},{9,13},{1... | collective-permute-start | bytes 2359304 | tf_op jit(solution)/shard_map/ppermute | solution.py:83
  140.4 0.9 copy-start.10
  141.3 2.3 %copy-start.9 = (bf16[768,512]{1,0:T(8,128)(2,1)}, bf16[768,512]{1,0:T(8,128)(2,1)S(1)}, u32[]{:S(2)}) copy-start(bf16[768,512]{1,0:T(8,128)(2,1)S(1)} %collective-permute-done.14.refs_22_) | copy-start | bytes 2359300
  141.3 19.8 %collective-permute-start.15 = (bf16[768,512]{1,0:T(8,128)(2,1)}, bf16[768,512]{1,0:T(8,128)(2,1)S(1)}, u32[]{:S(2)}, u32[]{:S(2)}) collective-permute-start(bf16[768,512]{1,0:T(8,128)(2,1)} %collective-permute-done.12.refs_21_), channel_id=1, source_target_pairs={{0,12},{1,13},{2,14},{3,15},{4,0},{5,1},{6,2},{7,3},{8,4},{9,5},{1... | collective-permute-start | bytes 2359304 | tf_op jit(solution)/shard_map/ppermute | solution.py:86
  141.6 19.5 %collective-permute-start.16 = (bf16[768,512]{1,0:T(8,128)(2,1)S(1)}, bf16[768,512]{1,0:T(8,128)(2,1)S(1)}, u32[]{:S(2)}, u32[]{:S(2)}) collective-permute-start(bf16[768,512]{1,0:T(8,128)(2,1)S(1)} %collective-permute-done.14.refs_22_), channel_id=1, source_target_pairs={{0,4},{1,5},{2,6},{3,7},{4,8},{5,9},{6,10},{7,11},{8,12},{9,13},{1... | collective-permute-start | bytes 2359304 | tf_op jit(solution)/shard_map/ppermute | solution.py:83
  143.6 17.5 %copy-start = (bf16[768,1024]{1,0:T(8,128)(2,1)S(1)}, bf16[768,1024]{1,0:T(8,128)(2,1)}, u32[]{:S(2)}) copy-start(bf16[768,1024]{1,0:T(8,128)(2,1)} %student_ref.1) | copy-start | bytes 4718596
  143.6 17.5 %copy-start.1 = (f32[8192]{0:T(1024)S(1)}, f32[8192]{0:T(1024)}, u32[]{:S(2)}) copy-start(f32[8192]{0:T(1024)} %param.6) | copy-start | bytes 98308
  143.7 17.5 %copy-start.2 = (s32[48]{0:T(128)S(1)}, s32[48]{0:T(128)}, u32[]{:S(2)}) copy-start(s32[48]{0:T(128)} %stack.151.plan_ref) | copy-start | bytes 580
  167.2 6.0 %collective-permute-start.17 = (f32[8,768]{1,0:T(8,128)S(1)}, f32[8,768]{1,0:T(8,128)S(1)}, u32[]{:S(2)}, u32[]{:S(2)}) collective-permute-start(f32[8,768]{1,0:T(8,128)S(1)} %get-tuple-element.36.own_ref), channel_id=1, source_target_pairs={{0,1},{1,0},{2,3},{3,2},{4,5},{5,4},{6,7},{7,6},{8,9},{9,8},{10,11... | collective-permute-start | bytes 73736 | tf_op jit(solution)/shard_map/ppermute | solution.py:401
  170.1 4.9 %collective-permute-start.18 = (f32[8,768]{1,0:T(8,128)S(1)}, f32[8,768]{1,0:T(8,128)S(1)}, u32[]{:S(2)}, u32[]{:S(2)}) collective-permute-start(f32[8,768]{1,0:T(8,128)S(1)} %get-tuple-element.36.own_ref), channel_id=1, source_target_pairs={{0,2},{1,3},{2,0},{3,1},{4,6},{5,7},{6,4},{7,5},{8,10},{9,11},{10,... | collective-permute-start | bytes 73736 | tf_op jit(solution)/shard_map/ppermute | solution.py:401
  170.1 5.6 %collective-permute-start.19 = (f32[8,768]{1,0:T(8,128)S(1)}, f32[8,768]{1,0:T(8,128)S(1)}, u32[]{:S(2)}, u32[]{:S(2)}) collective-permute-start(f32[8,768]{1,0:T(8,128)S(1)} %get-tuple-element.36.own_ref), channel_id=1, source_target_pairs={{0,3},{1,2},{2,1},{3,0},{4,7},{5,6},{6,5},{7,4},{8,11},{9,10},{10,... | collective-permute-start | bytes 73736 | tf_op jit(solution)/shard_map/ppermute | solution.py:401
  176.5 1.4 collective-permute-start.20
  177.8 10.5 %collective-permute-start.21 = (f32[1,128]{1,0:T(1,128)S(1)}, f32[1,128]{1,0:T(1,128)S(1)}, u32[]{:S(2)}, u32[]{:S(2)}) collective-permute-start(f32[1,128]{1,0:T(1,128)S(1)} %add.374), channel_id=1, source_target_pairs={{0,128},{16,144},{32,160},{48,176},{64,192},{80,208},{96,224},{112... | collective-permute-start | bytes 1544 | tf_op jit(solution)/shard_map/ppermute | solution.py:390
  188.3 5.6 %collective-permute-start.22 = (f32[1,128]{1,0:T(1,128)S(1)}, f32[1,128]{1,0:T(1,128)S(1)}, u32[]{:S(2)}, u32[]{:S(2)}) collective-permute-start(f32[1,128]{1,0:T(1,128)S(1)} %add.375), channel_id=1, source_target_pairs={{0,32},{16,48},{32,64},{48,80},{64,96},{80,112},{96,0},{112,16},{1... | collective-permute-start | bytes 1544 | tf_op jit(solution)/shard_map/ppermute | solution.py:390
  189.7 5.0 %collective-permute-start.23 = (f32[1,128]{1,0:T(1,128)S(1)}, f32[1,128]{1,0:T(1,128)S(1)}, u32[]{:S(2)}, u32[]{:S(2)}) collective-permute-start(f32[1,128]{1,0:T(1,128)S(1)} %add.375), channel_id=1, source_target_pairs={{0,64},{16,80},{32,96},{48,112},{64,0},{80,16},{96,32},{112,48},{1... | collective-permute-start | bytes 1544 | tf_op jit(solution)/shard_map/ppermute | solution.py:390
  192.8 3.5 %collective-permute-start.24 = (f32[1,128]{1,0:T(1,128)S(1)}, f32[1,128]{1,0:T(1,128)S(1)}, u32[]{:S(2)}, u32[]{:S(2)}) collective-permute-start(f32[1,128]{1,0:T(1,128)S(1)} %add.375), channel_id=1, source_target_pairs={{0,96},{16,112},{32,0},{48,16},{64,32},{80,48},{96,64},{112,80},{1... | collective-permute-start | bytes 1544 | tf_op jit(solution)/shard_map/ppermute | solution.py:390
  196.4 5.2 %collective-permute-start.25 = (f32[1,128]{1,0:T(1,128)S(1)}, f32[1,128]{1,0:T(1,128)S(1)}, u32[]{:S(2)}, u32[]{:S(2)}) collective-permute-start(f32[1,128]{1,0:T(1,128)S(1)} %add_add_fusion.1), channel_id=1, source_target_pairs={{0,4},{1,5},{2,6},{3,7},{4,8},{5,9},{6,10},{7,11},{8,12},{9,13},{1... | collective-permute-start | bytes 1544 | tf_op jit(solution)/shard_map/ppermute | solution.py:390
  197.9 5.0 %collective-permute-start.26 = (f32[1,128]{1,0:T(1,128)S(1)}, f32[1,128]{1,0:T(1,128)S(1)}, u32[]{:S(2)}, u32[]{:S(2)}) collective-permute-start(f32[1,128]{1,0:T(1,128)S(1)} %add_add_fusion.1), channel_id=1, source_target_pairs={{0,8},{1,9},{2,10},{3,11},{4,12},{5,13},{6,14},{7,15},{8,0},{9,1},... | collective-permute-start | bytes 1544 | tf_op jit(solution)/shard_map/ppermute | solution.py:390
  199.3 3.6 %collective-permute-start.27 = (f32[1,128]{1,0:T(1,128)S(1)}, f32[1,128]{1,0:T(1,128)S(1)}, u32[]{:S(2)}, u32[]{:S(2)}) collective-permute-start(f32[1,128]{1,0:T(1,128)S(1)} %add_add_fusion.1), channel_id=1, source_target_pairs={{0,12},{1,13},{2,14},{3,15},{4,0},{5,1},{6,2},{7,3},{8,4},{9,5},{1... | collective-permute-start | bytes 1544 | tf_op jit(solution)/shard_map/ppermute | solution.py:390
Sparse Core Ops, SparseCore 0:
  9.9 55.2 all-gather.4
  79.8 55.1 all-gather.6
